TPU v7x, 32 devices: a whole 2x2x4 slice. The times are simulated.
32 devices in a mesh: groups: 1, gx: 32 (over z, y, x, core).
Axes of the slice: x: 2, y: 2, z: 4, core: 2. Of those that a mesh axis runs over, the one named last changes fastest.
Arguments:
- solid_state: float32 [9, 2, 1, 256, 4, 128], P(None, None, 'groups', 'gx'), may hold values from -6 to 6
- water_state: float32 [4, 2, 1, 128, 12, 256], P(None, None, 'groups', 'gx'), may hold values from -6 to 6
- lame_lambda: float32 [256, 4, 128], P('gx'), may hold values from 0.4 to 1.2
- shear_mu: float32 [256, 4, 128], P('gx'), may hold values from 0.1 to 0.5
- solid_buoy: float32 [256, 4, 128], P('gx'), may hold values from 0.4 to 1
- water_kappa: float32 [128, 12, 256], P('gx'), may hold values from 0.5 to 1
- water_buoy: float32 [128, 12, 256], P('gx'), may hold values from 0.6 to 1.2
- seafloor: int32 [128, 256], P('gx'), may hold values from 6 to 12
- source_cell: int32 [1], P('groups'), may hold values from 0 to 196607
- wavelet: float32 [4, 1], P(None, 'groups'), may hold values from -48 to 48
- receiver_column: int32 [128], replicated, may hold values from 0 to 32767
- observed: float32 [4, 1, 128], P(None, 'groups'), may hold values from -6 to 6
Outputs:
- grad_lambda: float32 [256, 4, 128], P('gx', 'groups')
- grad_mu: float32 [256, 4, 128], P('gx', 'groups')
- grad_kappa: float32 [128, 12, 256], P('gx', 'groups')
- residuals: float32 [4, 1, 128], P(None, 'groups')
Inputs may be any that keep to these rules, and one draw needn't show every extreme that they name: Every column holds water from z = 0 to z = seafloor - 1 and rock below it. source_cell is (z * 128 + y) * 256 + x of a water cell with z below 6. receiver_column is y * 256 + x; two nodes may share a column.
All inputs are finite; a program needn't handle non-finite values.
Results may differ from a plain program's by a relative error of at most 0.00014.
Values sent between devices are 32-bit elements; how exact they have to be, the bound alone decides.
A program may use at most 64 MiB of HBM per device.

v0:
```python
import jax
import jax.numpy as jnp
from jax import lax
from jax.sharding import PartitionSpec as P

COEFF = (1225.0 / 1024.0, -245.0 / 3072.0, 49.0 / 5120.0, -5.0 / 7168.0)
TIME_STEP = 0.2


def with_halo(array, sides, width):
    for axis, dim in sides:
        devices, length = (lax.axis_size(axis), array.shape[dim])
        up = [(i, (i + 1) % devices) for i in range(devices - 1)]
        down = [(j, i) for i, j in up]
        last = lax.slice_in_dim(array, length - width, length, axis=dim)
        first = lax.slice_in_dim(array, 0, width, axis=dim)
        before = lax.ppermute(last, axis, up)
        after = lax.ppermute(first, axis, down)
        array = jnp.concatenate([before, array, after], axis=dim)
    return array


def stencil(padded, axis, forward):
    length = padded.shape[axis] - 8
    summed = None
    for offset in range(1, 5):
        if forward:
            front_at, back_at = (4 + offset, 5 - offset)
        else:
            front_at, back_at = (3 + offset, 4 - offset)
        front = lax.slice_in_dim(padded, front_at, front_at + length, axis=axis)
        back = lax.slice_in_dim(padded, back_at, back_at + length, axis=axis)
        addend = COEFF[offset - 1] * (front - back)
        summed = addend if summed is None else summed + addend
    return summed


def padded_zero(field, axis):
    widths = [(0, 0)] * field.ndim
    widths[axis] = (4, 4)
    return jnp.pad(field, widths)


def derive(field, axis, forward):
    return stencil(padded_zero(field, axis), axis, forward)


def on_device(
    solid_state,
    water_state,
    lame_lambda,
    shear_mu,
    solid_buoy,
    water_kappa,
    water_buoy,
    seafloor,
    source_cell,
    wavelet,
    receiver_column,
    observed,
):
    parts = lax.axis_size("gx")
    place = lax.axis_index("gx")
    width_x = solid_state.shape[3]
    total_y = solid_state.shape[5]
    total_x = width_x * parts
    shots = solid_state.shape[2]
    shard_axis = 2
    anchor_y = place * water_state.shape[3]
    anchor_x = 0

    def water_halo(field):
        return with_halo(field, (("gx", 2),), 4)

    def water_derive(field, axis, forward):
        if axis == shard_axis:
            return stencil(water_halo(field), axis, forward)
        return derive(field, axis, forward)

    def solid_halo(stacked):
        return with_halo(stacked, (("gx", 3),), 4)

    vel_x, vel_y, vel_z = (solid_state[0], solid_state[1], solid_state[2])
    sig_xx, sig_yy, sig_zz = (solid_state[3], solid_state[4], solid_state[5])
    sig_xy, sig_xz, sig_yz = (solid_state[6], solid_state[7], solid_state[8])
    pressure, flow_x, flow_y, flow_z = (
        water_state[0],
        water_state[1],
        water_state[2],
        water_state[3],
    )
    local_y = pressure.shape[2]
    depth_rows = pressure.shape[3]
    local_x = pressure.shape[4]
    depth_idx = lax.broadcasted_iota(jnp.int32, (1, depth_rows, 1), 1)
    floor_rows = seafloor[:, None, :]
    live = (depth_idx < floor_rows).astype(jnp.float32)
    bottom = (depth_idx == floor_rows - 1).astype(jnp.float32)
    above = (depth_idx < floor_rows - 1).astype(jnp.float32)
    rows_y = lax.broadcasted_iota(jnp.int32, (local_y, 1, 1), 0) + anchor_y
    cols_x = lax.broadcasted_iota(jnp.int32, (1, 1, local_x), 2) + anchor_x
    flat_cell = (depth_idx * total_y + rows_y) * total_x + cols_x
    source_hot = (flat_cell[None] == source_cell[:, None, None, None]).astype(jnp.float32)
    node_y = receiver_column // total_x
    node_x = receiver_column % total_x
    inside = (
        (node_y >= anchor_y)
        & (node_y < anchor_y + local_y)
        & (node_x >= anchor_x)
        & (node_x < anchor_x + local_x)
    )
    local_col = (node_y - anchor_y) * local_x + (node_x - anchor_x)
    column_iota = lax.broadcasted_iota(jnp.int32, (1, local_y * local_x), 1)
    node_hot = ((column_iota == local_col[:, None]) & inside[:, None]).astype(jnp.float32)
    grad_lambda = jnp.zeros(lame_lambda.shape, jnp.float32)
    grad_mu = jnp.zeros(lame_lambda.shape, jnp.float32)
    grad_kappa = jnp.zeros(water_kappa.shape, jnp.float32)
    misfits = []
    for step in range(wavelet.shape[0]):
        floor_pressure = jnp.sum(pressure * bottom, axis=3)
        stress_pad = solid_halo(jnp.stack([sig_xx, sig_xy, sig_xz]))
        vel_x = vel_x + TIME_STEP * solid_buoy * (
            stencil(stress_pad[0], 2, True) + derive(sig_xy, 4, False) + derive(sig_xz, 3, False)
        )
        vel_y = vel_y + TIME_STEP * solid_buoy * (
            stencil(stress_pad[1], 2, False) + derive(sig_yy, 4, True) + derive(sig_yz, 3, False)
        )
        vel_z = vel_z + TIME_STEP * solid_buoy * (
            stencil(stress_pad[2], 2, False) + derive(sig_yz, 4, False) + derive(sig_zz, 3, True)
        )
        floor_velocity = lax.all_to_all(
            jnp.transpose(vel_z[:, :, :, 0, :], (0, 1, 3, 2)),
            "gx",
            split_axis=2,
            concat_axis=3,
            tiled=True,
        )
        flow_x = (flow_x - TIME_STEP * water_buoy * water_derive(pressure, 4, True)) * live
        flow_y = (flow_y - TIME_STEP * water_buoy * water_derive(pressure, 2, True)) * live
        flow_z = (
            flow_z - TIME_STEP * water_buoy * derive(pressure, 3, True)
        ) * above + floor_velocity[:, :, :, None, :] * bottom
        velocity_pad = solid_halo(jnp.stack([vel_x, vel_y, vel_z]))
        strain_x = stencil(velocity_pad[0], 2, False)
        strain_y = derive(vel_y, 4, False)
        strain_z = derive(vel_z, 3, False)
        dilation = strain_x + strain_y + strain_z
        shear_xy = derive(vel_x, 4, True) + stencil(velocity_pad[1], 2, True)
        shear_xz = derive(vel_x, 3, True) + stencil(velocity_pad[2], 2, True)
        shear_yz = derive(vel_y, 3, True) + derive(vel_z, 4, True)
        lam_part = lame_lambda * dilation
        sig_xx = sig_xx + TIME_STEP * (lam_part + 2.0 * shear_mu * strain_x)
        sig_yy = sig_yy + TIME_STEP * (lam_part + 2.0 * shear_mu * strain_y)
        sig_zz = sig_zz + TIME_STEP * (lam_part + 2.0 * shear_mu * strain_z)
        sig_xy = sig_xy + TIME_STEP * shear_mu * shear_xy
        sig_xz = sig_xz + TIME_STEP * shear_mu * shear_xz
        sig_yz = sig_yz + TIME_STEP * shear_mu * shear_yz
        rock_pressure = jnp.transpose(
            lax.all_to_all(floor_pressure, "gx", split_axis=3, concat_axis=2, tiled=True),
            (0, 1, 3, 2),
        )
        sig_zz = sig_zz.at[:, :, :, 0, :].set(-rock_pressure)
        grad_lambda = grad_lambda + jnp.sum(dilation[0] * dilation[1], axis=0)
        normal_part = (
            strain_x[0] * strain_x[1] + strain_y[0] * strain_y[1] + strain_z[0] * strain_z[1]
        )
        shear_part = (
            shear_xy[0] * shear_xy[1] + shear_xz[0] * shear_xz[1] + shear_yz[0] * shear_yz[1]
        )
        grad_mu = grad_mu + jnp.sum(2.0 * normal_part + shear_part, axis=0)
        pressure = (
            pressure
            - TIME_STEP
            * water_kappa
            * (
                water_derive(flow_x, 4, False)
                + water_derive(flow_y, 2, False)
                + derive(flow_z, 3, False)
            )
        ) * live
        pressure = pressure.at[0].add(wavelet[step][:, None, None, None] * source_hot)
        surface = jnp.sum(pressure * bottom, axis=3)
        partial_record = jnp.einsum(
            "sc,rc->sr",
            surface[0].reshape(shots, local_y * local_x),
            node_hot,
            precision=lax.Precision.HIGHEST,
        )
        recorded = lax.psum(partial_record, "gx")
        misfit = recorded - observed[step]
        scaled = misfit * lax.rsqrt(jnp.mean(misfit * misfit, axis=1, keepdims=True) + 1e-06)
        inject = jnp.dot(
            scaled, node_hot, precision=lax.Precision.HIGHEST, preferred_element_type=jnp.float32
        ).reshape(shots, local_y, local_x)
        pressure = pressure.at[1].add(inject[:, :, None, :] * bottom)
        grad_kappa = grad_kappa + jnp.sum(pressure[0] * pressure[1], axis=0)
        misfits.append(misfit)
    return (grad_lambda, grad_mu, grad_kappa, jnp.stack(misfits))


def solution(mesh):
    placed = (
        P(None, None, "groups", "gx", None, None),
        P(None, None, "groups", "gx", None, None),
        P("gx", None, None),
        P("gx", None, None),
        P("gx", None, None),
        P("gx", None, None),
        P("gx", None, None),
        P("gx", None),
        P("groups"),
        P(None, "groups"),
        P(),
        P(None, "groups", None),
    )
    return jax.shard_map(
        on_device,
        mesh=mesh,
        in_specs=placed,
        out_specs=(
            P("gx", "groups", None),
            P("gx", "groups", None),
            P("gx", "groups", None),
            P(None, "groups", None),
        ),
        check_vma=False,
    )
```

profile of v0, /device:TPU:0, one launch (start us, length us, event | category | flops | bytes accessed | tf_op | source)
XLA Modules:
  0.0 367.0 jit_solution(11349562170741559003)
XLA Ops:
  0.6 0.9 slice_bitcast_fusion.3
  1.6 1.3 collective-permute-start.10
  2.9 3.0 collective-permute-start.11
  5.9 0.8 slice.2874
  6.8 1.3 collective-permute-start.1
  8.1 5.1 %collective-permute-start = (f32[3,2,1,4,4,128]{5,4,3,2,1,0:T(4,128)S(1)}, f32[3,2,1,4,4,128]{5,4,3,2,1,0:T(4,128)S(1)}, u32[]{:S(2)}, u32[]{:S(2)}) collective-permute-start(f32[3,2,1,4,4,128]{5,4,3,2,1,0:T(4,128)S(1)} %get-tuple-element.248), channel_id=1, source_target_pairs={{0,1},{1,2},{2,3},{3,4},{4,5},{5,6},{6,7},{7,8},{8,9},{9,10},{10,1... | collective-permute-start | bytes 147464 | tf_op jit(solution)/shard_map/ppermute | solution.py:17
  14.7 0.8 copy-done.3
  15.5 0.8 copy-done.4
  18.7 0.8 copy.963
  19.5 9.7 %all-to-all-start.1 = ((f32[2,1,128,8]{3,0,1,2:T(2,128)}), f32[2,1,128,8]{3,0,1,2:T(2,128)S(1)}, u32[]{:S(2)}, u32[]{:S(2)}) async-start(f32[2,1,128,8]{3,0,1,2:T(2,128)} %copy.963), calls=%async_computation.1 | async-start | bytes 262144 | tf_op jit(solution)/shard_map/all_to_all | solution.py:131
  29.7 1.4 collective-permute-start.3
  31.2 3.0 collective-permute-start.2
  34.2 3.3 all-to-all-done.1
  39.1 1.3 collective-permute-start.5
  40.4 3.0 collective-permute-start.4
  43.9 3.4 collective-permute-start.12
  47.3 1.3 collective-permute-start.13
  49.1 1.4 collective-permute-done.13
  51.0 0.7 fusion.377
  51.8 0.9 copy.948
  52.6 12.4 %all-to-all-start = ((f32[2,1,4,256]{2,0,1,3:T(2,128)}), f32[2,1,4,256]{2,0,1,3:T(2,128)S(1)}, u32[]{:S(2)}, u32[]{:S(2)}) async-start(f32[2,1,4,256]{2,0,1,3:T(2,128)} %copy.948), calls=%async_computation | async-start | bytes 524288 | tf_op jit(solution)/shard_map/all_to_all | solution.py:159
  65.5 40.5 %psum.28 = f32[1,128]{1,0:T(1,128)S(1)} all-reduce(f32[1,128]{1,0:T(1,128)S(1)} %fusion.7), channel_id=1, replica_groups=mesh['groups'=1,'gx'=32] {'gx'}, use_global_device_ids=true, to_apply=%region_2.3 | all-reduce | flops 128 | bytes 1024 | tf_op jit(solution)/shard_map/psum | solution.py:189
  107.8 1.3 collective-permute-start.18
  109.1 3.0 collective-permute-start.19
  112.8 0.8 copy.978
  113.6 6.2 %all-to-all-start.3 = ((f32[2,1,128,8]{3,0,1,2:T(2,128)}), f32[2,1,128,8]{3,0,1,2:T(2,128)S(1)}, u32[]{:S(2)}, u32[]{:S(2)}) async-start(f32[2,1,128,8]{3,0,1,2:T(2,128)} %copy.978), calls=%async_computation.3 | async-start | bytes 262144 | tf_op jit(solution)/shard_map/all_to_all | solution.py:131
  119.9 1.3 collective-permute-start.7
  121.2 3.0 collective-permute-start.6
  124.2 3.8 %all-to-all-done.3 = f32[2,1,128,8]{3,0,1,2:T(2,128)S(1)} async-done(((f32[2,1,128,8]{3,0,1,2:T(2,128)}), f32[2,1,128,8]{3,0,1,2:T(2,128)S(1)}, u32[]{:S(2)}, u32[]{:S(2)}) %all-to-all-start.3) | async-done | bytes 8224 | tf_op jit(solution)/shard_map/all_to_all | solution.py:131
  129.1 1.3 collective-permute-start.9
  130.4 3.0 collective-permute-start.8
  133.9 3.4 collective-permute-start.20
  137.3 1.3 collective-permute-start.21
  139.1 1.4 collective-permute-done.21
  141.8 0.9 copy.966
  142.7 11.9 %all-to-all-start.2 = ((f32[2,1,4,256]{2,0,1,3:T(2,128)}), f32[2,1,4,256]{2,0,1,3:T(2,128)S(1)}, u32[]{:S(2)}, u32[]{:S(2)}) async-start(f32[2,1,4,256]{2,0,1,3:T(2,128)} %copy.966), calls=%async_computation.2 | async-start | bytes 524288 | tf_op jit(solution)/shard_map/all_to_all | solution.py:159
  155.0 40.5 %psum.29 = f32[1,128]{1,0:T(1,128)S(1)} all-reduce(f32[1,128]{1,0:T(1,128)S(1)} %fusion.5), channel_id=1, replica_groups=mesh['groups'=1,'gx'=32] {'gx'}, use_global_device_ids=true, to_apply=%region_6.7 | all-reduce | flops 128 | bytes 1024 | tf_op jit(solution)/shard_map/psum | solution.py:189
  197.3 1.3 collective-permute-start.24
  198.6 3.0 collective-permute-start.25
  202.3 0.8 copy.989
  203.1 6.2 %all-to-all-start.5 = ((f32[2,1,128,8]{3,0,1,2:T(2,128)}), f32[2,1,128,8]{3,0,1,2:T(2,128)S(1)}, u32[]{:S(2)}, u32[]{:S(2)}) async-start(f32[2,1,128,8]{3,0,1,2:T(2,128)} %copy.989), calls=%async_computation.5 | async-start | bytes 262144 | tf_op jit(solution)/shard_map/all_to_all | solution.py:131
  209.4 1.3 collective-permute-start.15
  210.7 3.0 collective-permute-start.14
  213.7 3.8 %all-to-all-done.5 = f32[2,1,128,8]{3,0,1,2:T(2,128)S(1)} async-done(((f32[2,1,128,8]{3,0,1,2:T(2,128)}), f32[2,1,128,8]{3,0,1,2:T(2,128)S(1)}, u32[]{:S(2)}, u32[]{:S(2)}) %all-to-all-start.5) | async-done | bytes 8224 | tf_op jit(solution)/shard_map/all_to_all | solution.py:131
  218.6 1.3 collective-permute-start.17
  219.9 3.0 collective-permute-start.16
  223.4 3.4 collective-permute-start.26
  226.8 1.3 collective-permute-start.27
  228.6 1.4 collective-permute-done.27
  231.3 0.9 copy.981
  232.2 11.9 %all-to-all-start.4 = ((f32[2,1,4,256]{2,0,1,3:T(2,128)}), f32[2,1,4,256]{2,0,1,3:T(2,128)S(1)}, u32[]{:S(2)}, u32[]{:S(2)}) async-start(f32[2,1,4,256]{2,0,1,3:T(2,128)} %copy.981), calls=%async_computation.4 | async-start | bytes 524288 | tf_op jit(solution)/shard_map/all_to_all | solution.py:159
  244.5 40.5 %psum.30 = f32[1,128]{1,0:T(1,128)S(1)} all-reduce(f32[1,128]{1,0:T(1,128)S(1)} %fusion.3), channel_id=1, replica_groups=mesh['groups'=1,'gx'=32] {'gx'}, use_global_device_ids=true, to_apply=%region_10.11 | all-reduce | flops 128 | bytes 1024 | tf_op jit(solution)/shard_map/psum | solution.py:189
  286.8 1.3 collective-permute-start.28
  288.1 3.0 collective-permute-start.29
  291.8 0.8 copy.992
  292.6 6.2 %all-to-all-start.6 = ((f32[2,1,128,8]{3,0,1,2:T(2,128)}), f32[2,1,128,8]{3,0,1,2:T(2,128)S(1)}, u32[]{:S(2)}, u32[]{:S(2)}) async-start(f32[2,1,128,8]{3,0,1,2:T(2,128)} %copy.992), calls=%async_computation.6 | async-start | bytes 262144 | tf_op jit(solution)/shard_map/all_to_all | solution.py:131
  298.9 1.3 collective-permute-start.23
  300.2 3.0 collective-permute-start.22
  303.2 3.8 %all-to-all-done.6 = f32[2,1,128,8]{3,0,1,2:T(2,128)S(1)} async-done(((f32[2,1,128,8]{3,0,1,2:T(2,128)}), f32[2,1,128,8]{3,0,1,2:T(2,128)S(1)}, u32[]{:S(2)}, u32[]{:S(2)}) %all-to-all-start.6) | async-done | bytes 8224 | tf_op jit(solution)/shard_map/all_to_all | solution.py:131
  309.1 2.1 collective-permute-start.30
  311.2 1.3 collective-permute-start.31
  313.2 1.9 collective-permute-done.31
  316.8 46.5 %psum.31 = f32[1,128]{1,0:T(1,128)S(1)} all-reduce(f32[1,128]{1,0:T(1,128)S(1)} %fusion.1), channel_id=1, replica_groups=mesh['groups'=1,'gx'=32] {'gx'}, use_global_device_ids=true, to_apply=%region_13.14 | all-reduce | flops 128 | bytes 1024 | tf_op jit(solution)/shard_map/psum | solution.py:189
  365.1 1.4 fusion.372
  (210 shorter events, 25.5 us)
Async XLA Ops:
  0.6 6.1 %copy-start = (f32[9,2,1,8,4,128]{5,4,3,2,1,0:T(4,128)S(1)}, f32[9,2,1,8,4,128]{5,4,3,2,1,0:T(4,128)}, u32[]{:S(2)}) copy-start(f32[9,2,1,8,4,128]{5,4,3,2,1,0:T(4,128)} %param.34) | copy-start | bytes 884740
  1.6 41.8 %collective-permute-start.10 = (f32[2,1,4,12,256]{4,2,3,1,0:T(4,128)S(1)}, f32[2,1,4,12,256]{4,2,3,1,0:T(4,128)S(1)}, u32[]{:S(2)}, u32[]{:S(2)}) collective-permute-start(f32[2,1,4,12,256]{4,2,3,1,0:T(4,128)S(1)} %slice_bitcast_fusion.3), channel_id=1, source_target_pairs={{1,0},{2,1},{3,2},{4,3},{5,4},{6,5},{7,6},{8,7},{9,8},{10,9},{11,1... | collective-permute-start | bytes 294920 | tf_op jit(solution)/shard_map/ppermute | solution.py:18
  2.9 40.5 %collective-permute-start.11 = (f32[2,1,4,12,256]{4,2,3,1,0:T(4,128)S(1)}, f32[2,1,4,12,256]{4,2,3,1,0:T(4,128)S(1)}, u32[]{:S(2)}, u32[]{:S(2)}) collective-permute-start(f32[2,1,4,12,256]{4,2,3,1,0:T(4,128)S(1)} %slice_bitcast_fusion.3), channel_id=1, source_target_pairs={{0,1},{1,2},{2,3},{3,4},{4,5},{5,6},{6,7},{7,8},{8,9},{9,10},{10,1... | collective-permute-start | bytes 294920 | tf_op jit(solution)/shard_map/ppermute | solution.py:17
  6.8 6.4 %copy-start.7 = (s32[4,256]{1,0:T(4,128)S(1)}, s32[4,256]{1,0:T(4,128)}, u32[]{:S(2)}) copy-start(s32[4,256]{1,0:T(4,128)} %param.41) | copy-start | bytes 12292
  6.8 11.5 %collective-permute-start.1 = (f32[3,2,1,4,4,128]{5,4,3,2,1,0:T(4,128)S(1)}, f32[3,2,1,4,4,128]{5,4,3,2,1,0:T(4,128)S(1)}, u32[]{:S(2)}, u32[]{:S(2)}) collective-permute-start(f32[3,2,1,4,4,128]{5,4,3,2,1,0:T(4,128)S(1)} %get-tuple-element.249), channel_id=1, source_target_pairs={{1,0},{2,1},{3,2},{4,3},{5,4},{6,5},{7,6},{8,7},{9,8},{10,9},{11,1... | collective-permute-start | bytes 147464 | tf_op jit(solution)/shard_map/ppermute | solution.py:18
  8.1 10.3 %collective-permute-start = (f32[3,2,1,4,4,128]{5,4,3,2,1,0:T(4,128)S(1)}, f32[3,2,1,4,4,128]{5,4,3,2,1,0:T(4,128)S(1)}, u32[]{:S(2)}, u32[]{:S(2)}) collective-permute-start(f32[3,2,1,4,4,128]{5,4,3,2,1,0:T(4,128)S(1)} %get-tuple-element.248), channel_id=1, source_target_pairs={{0,1},{1,2},{2,3},{3,4},{4,5},{5,6},{6,7},{7,8},{8,9},{9,10},{10,1... | collective-permute-start | bytes 147464 | tf_op jit(solution)/shard_map/ppermute | solution.py:17
  13.3 0.7 copy-start.6
  14.0 0.7 copy-start.5
  14.7 0.8 copy-start.3
  15.5 0.8 copy-start.4
  16.3 0.7 copy-start.8
  17.0 0.7 copy-start.9
  19.5 18.0 %all-to-all-start.1 = ((f32[2,1,128,8]{3,0,1,2:T(2,128)}), f32[2,1,128,8]{3,0,1,2:T(2,128)S(1)}, u32[]{:S(2)}, u32[]{:S(2)}) async-start(f32[2,1,128,8]{3,0,1,2:T(2,128)} %copy.963), calls=%async_computation.1 | async-start | bytes 262144 | tf_op jit(solution)/shard_map/all_to_all | solution.py:131
  29.7 8.0 %copy-start.1 = (f32[4,2,1,4,12,256]{5,3,4,2,1,0:T(4,128)S(1)}, f32[4,2,1,4,12,256]{5,3,4,2,1,0:T(4,128)}, u32[]{:S(2)}) copy-start(f32[4,2,1,4,12,256]{5,3,4,2,1,0:T(4,128)} %param.35) | copy-start | bytes 1179652
  29.7 8.0 %collective-permute-start.3 = (f32[3,2,1,4,4,128]{5,4,3,2,1,0:T(4,128)S(1)}, f32[3,2,1,4,4,128]{5,4,3,2,1,0:T(4,128)S(1)}, u32[]{:S(2)}, u32[]{:S(2)}) collective-permute-start(f32[3,2,1,4,4,128]{5,4,3,2,1,0:T(4,128)S(1)} %get-tuple-element.247), channel_id=1, source_target_pairs={{1,0},{2,1},{3,2},{4,3},{5,4},{6,5},{7,6},{8,7},{9,8},{10,9},{11,1... | collective-permute-start | bytes 147464 | tf_op jit(solution)/shard_map/ppermute | solution.py:18
  31.2 6.6 %collective-permute-start.2 = (f32[3,2,1,4,4,128]{5,4,3,2,1,0:T(4,128)S(1)}, f32[3,2,1,4,4,128]{5,4,3,2,1,0:T(4,128)S(1)}, u32[]{:S(2)}, u32[]{:S(2)}) collective-permute-start(f32[3,2,1,4,4,128]{5,4,3,2,1,0:T(4,128)S(1)} %get-tuple-element.246), channel_id=1, source_target_pairs={{0,1},{1,2},{2,3},{3,4},{4,5},{5,6},{6,7},{7,8},{8,9},{9,10},{10,1... | collective-permute-start | bytes 147464 | tf_op jit(solution)/shard_map/ppermute | solution.py:17
  37.9 0.7 copy-start.2
  39.1 9.5 %collective-permute-start.5 = (f32[3,2,1,4,4,128]{5,4,3,2,1,0:T(4,128)S(1)}, f32[3,2,1,4,4,128]{5,4,3,2,1,0:T(4,128)S(1)}, u32[]{:S(2)}, u32[]{:S(2)}) collective-permute-start(f32[3,2,1,4,4,128]{5,4,3,2,1,0:T(4,128)S(1)} %get-tuple-element.245), channel_id=1, source_target_pairs={{1,0},{2,1},{3,2},{4,3},{5,4},{6,5},{7,6},{8,7},{9,8},{10,9},{11,1... | collective-permute-start | bytes 147464 | tf_op jit(solution)/shard_map/ppermute | solution.py:18
  40.4 8.2 %collective-permute-start.4 = (f32[3,2,1,4,4,128]{5,4,3,2,1,0:T(4,128)S(1)}, f32[3,2,1,4,4,128]{5,4,3,2,1,0:T(4,128)S(1)}, u32[]{:S(2)}, u32[]{:S(2)}) collective-permute-start(f32[3,2,1,4,4,128]{5,4,3,2,1,0:T(4,128)S(1)} %get-tuple-element.244), channel_id=1, source_target_pairs={{0,1},{1,2},{2,3},{3,4},{4,5},{5,6},{6,7},{7,8},{8,9},{9,10},{10,1... | collective-permute-start | bytes 147464 | tf_op jit(solution)/shard_map/ppermute | solution.py:17
  43.9 5.2 %collective-permute-start.12 = (f32[2,1,4,12,256]{4,2,3,1,0:T(4,128)S(1)}, f32[2,1,4,12,256]{4,2,3,1,0:T(4,128)S(1)}, u32[]{:S(2)}, u32[]{:S(2)}) collective-permute-start(f32[2,1,4,12,256]{4,2,3,1,0:T(4,128)S(1)} %get-tuple-element.190), channel_id=1, source_target_pairs={{0,1},{1,2},{2,3},{3,4},{4,5},{5,6},{6,7},{7,8},{8,9},{9,10},{10,1... | collective-permute-start | bytes 294920 | tf_op jit(solution)/shard_map/ppermute | solution.py:17
  47.3 3.2 collective-permute-start.13
  52.6 59.5 %all-to-all-start = ((f32[2,1,4,256]{2,0,1,3:T(2,128)}), f32[2,1,4,256]{2,0,1,3:T(2,128)S(1)}, u32[]{:S(2)}, u32[]{:S(2)}) async-start(f32[2,1,4,256]{2,0,1,3:T(2,128)} %copy.948), calls=%async_computation | async-start | bytes 524288 | tf_op jit(solution)/shard_map/all_to_all | solution.py:159
  65.1 40.9 %copy-start.10 = (f32[4,1,128]{2,1,0:T(1,128)S(1)}, f32[4,1,128]{2,1,0:T(1,128)}, u32[]{:S(2)}) copy-start(f32[4,1,128]{2,1,0:T(1,128)} %param.45) | copy-start | bytes 6148
  107.8 25.7 %collective-permute-start.18 = (f32[2,1,4,12,256]{4,2,3,1,0:T(4,128)S(1)}, f32[2,1,4,12,256]{4,2,3,1,0:T(4,128)S(1)}, u32[]{:S(2)}, u32[]{:S(2)}) collective-permute-start(f32[2,1,4,12,256]{4,2,3,1,0:T(4,128)S(1)} %fusion.1104), channel_id=1, source_target_pairs={{1,0},{2,1},{3,2},{4,3},{5,4},{6,5},{7,6},{8,7},{9,8},{10,9},{11,1... | collective-permute-start | bytes 294920 | tf_op jit(solution)/shard_map/ppermute | solution.py:18
  109.1 24.4 %collective-permute-start.19 = (f32[2,1,4,12,256]{4,2,3,1,0:T(4,128)S(1)}, f32[2,1,4,12,256]{4,2,3,1,0:T(4,128)S(1)}, u32[]{:S(2)}, u32[]{:S(2)}) collective-permute-start(f32[2,1,4,12,256]{4,2,3,1,0:T(4,128)S(1)} %fusion.1104), channel_id=1, source_target_pairs={{0,1},{1,2},{2,3},{3,4},{4,5},{5,6},{6,7},{7,8},{8,9},{9,10},{10,1... | collective-permute-start | bytes 294920 | tf_op jit(solution)/shard_map/ppermute | solution.py:17
  113.6 14.4 %all-to-all-start.3 = ((f32[2,1,128,8]{3,0,1,2:T(2,128)}), f32[2,1,128,8]{3,0,1,2:T(2,128)S(1)}, u32[]{:S(2)}, u32[]{:S(2)}) async-start(f32[2,1,128,8]{3,0,1,2:T(2,128)} %copy.978), calls=%async_computation.3 | async-start | bytes 262144 | tf_op jit(solution)/shard_map/all_to_all | solution.py:131
  119.9 8.4 %collective-permute-start.7 = (f32[3,2,1,4,4,128]{5,4,3,2,1,0:T(4,128)S(1)}, f32[3,2,1,4,4,128]{5,4,3,2,1,0:T(4,128)S(1)}, u32[]{:S(2)}, u32[]{:S(2)}) collective-permute-start(f32[3,2,1,4,4,128]{5,4,3,2,1,0:T(4,128)S(1)} %get-tuple-element.243), channel_id=1, source_target_pairs={{1,0},{2,1},{3,2},{4,3},{5,4},{6,5},{7,6},{8,7},{9,8},{10,9},{11,1... | collective-permute-start | bytes 147464 | tf_op jit(solution)/shard_map/ppermute | solution.py:18
  121.2 7.2 %collective-permute-start.6 = (f32[3,2,1,4,4,128]{5,4,3,2,1,0:T(4,128)S(1)}, f32[3,2,1,4,4,128]{5,4,3,2,1,0:T(4,128)S(1)}, u32[]{:S(2)}, u32[]{:S(2)}) collective-permute-start(f32[3,2,1,4,4,128]{5,4,3,2,1,0:T(4,128)S(1)} %get-tuple-element.242), channel_id=1, source_target_pairs={{0,1},{1,2},{2,3},{3,4},{4,5},{5,6},{6,7},{7,8},{8,9},{9,10},{10,1... | collective-permute-start | bytes 147464 | tf_op jit(solution)/shard_map/ppermute | solution.py:17
  129.1 9.5 %collective-permute-start.9 = (f32[3,2,1,4,4,128]{5,4,3,2,1,0:T(4,128)S(1)}, f32[3,2,1,4,4,128]{5,4,3,2,1,0:T(4,128)S(1)}, u32[]{:S(2)}, u32[]{:S(2)}) collective-permute-start(f32[3,2,1,4,4,128]{5,4,3,2,1,0:T(4,128)S(1)} %get-tuple-element.241), channel_id=1, source_target_pairs={{1,0},{2,1},{3,2},{4,3},{5,4},{6,5},{7,6},{8,7},{9,8},{10,9},{11,1... | collective-permute-start | bytes 147464 | tf_op jit(solution)/shard_map/ppermute | solution.py:18
  130.4 8.2 %collective-permute-start.8 = (f32[3,2,1,4,4,128]{5,4,3,2,1,0:T(4,128)S(1)}, f32[3,2,1,4,4,128]{5,4,3,2,1,0:T(4,128)S(1)}, u32[]{:S(2)}, u32[]{:S(2)}) collective-permute-start(f32[3,2,1,4,4,128]{5,4,3,2,1,0:T(4,128)S(1)} %get-tuple-element.240), channel_id=1, source_target_pairs={{0,1},{1,2},{2,3},{3,4},{4,5},{5,6},{6,7},{7,8},{8,9},{9,10},{10,1... | collective-permute-start | bytes 147464 | tf_op jit(solution)/shard_map/ppermute | solution.py:17
  133.9 5.2 %collective-permute-start.20 = (f32[2,1,4,12,256]{4,2,3,1,0:T(4,128)S(1)}, f32[2,1,4,12,256]{4,2,3,1,0:T(4,128)S(1)}, u32[]{:S(2)}, u32[]{:S(2)}) collective-permute-start(f32[2,1,4,12,256]{4,2,3,1,0:T(4,128)S(1)} %get-tuple-element.220), channel_id=1, source_target_pairs={{0,1},{1,2},{2,3},{3,4},{4,5},{5,6},{6,7},{7,8},{8,9},{9,10},{10,1... | collective-permute-start | bytes 294920 | tf_op jit(solution)/shard_map/ppermute | solution.py:17
  137.3 3.2 collective-permute-start.21
  142.7 59.0 %all-to-all-start.2 = ((f32[2,1,4,256]{2,0,1,3:T(2,128)}), f32[2,1,4,256]{2,0,1,3:T(2,128)S(1)}, u32[]{:S(2)}, u32[]{:S(2)}) async-start(f32[2,1,4,256]{2,0,1,3:T(2,128)} %copy.966), calls=%async_computation.2 | async-start | bytes 524288 | tf_op jit(solution)/shard_map/all_to_all | solution.py:159
  197.3 25.7 %collective-permute-start.24 = (f32[2,1,4,12,256]{4,2,3,1,0:T(4,128)S(1)}, f32[2,1,4,12,256]{4,2,3,1,0:T(4,128)S(1)}, u32[]{:S(2)}, u32[]{:S(2)}) collective-permute-start(f32[2,1,4,12,256]{4,2,3,1,0:T(4,128)S(1)} %fusion.1105), channel_id=1, source_target_pairs={{1,0},{2,1},{3,2},{4,3},{5,4},{6,5},{7,6},{8,7},{9,8},{10,9},{11,1... | collective-permute-start | bytes 294920 | tf_op jit(solution)/shard_map/ppermute | solution.py:18
  198.6 24.4 %collective-permute-start.25 = (f32[2,1,4,12,256]{4,2,3,1,0:T(4,128)S(1)}, f32[2,1,4,12,256]{4,2,3,1,0:T(4,128)S(1)}, u32[]{:S(2)}, u32[]{:S(2)}) collective-permute-start(f32[2,1,4,12,256]{4,2,3,1,0:T(4,128)S(1)} %fusion.1105), channel_id=1, source_target_pairs={{0,1},{1,2},{2,3},{3,4},{4,5},{5,6},{6,7},{7,8},{8,9},{9,10},{10,1... | collective-permute-start | bytes 294920 | tf_op jit(solution)/shard_map/ppermute | solution.py:17
  203.1 14.4 %all-to-all-start.5 = ((f32[2,1,128,8]{3,0,1,2:T(2,128)}), f32[2,1,128,8]{3,0,1,2:T(2,128)S(1)}, u32[]{:S(2)}, u32[]{:S(2)}) async-start(f32[2,1,128,8]{3,0,1,2:T(2,128)} %copy.989), calls=%async_computation.5 | async-start | bytes 262144 | tf_op jit(solution)/shard_map/all_to_all | solution.py:131
  209.4 8.4 %collective-permute-start.15 = (f32[3,2,1,4,4,128]{5,4,3,2,1,0:T(4,128)S(1)}, f32[3,2,1,4,4,128]{5,4,3,2,1,0:T(4,128)S(1)}, u32[]{:S(2)}, u32[]{:S(2)}) collective-permute-start(f32[3,2,1,4,4,128]{5,4,3,2,1,0:T(4,128)S(1)} %get-tuple-element.239), channel_id=1, source_target_pairs={{1,0},{2,1},{3,2},{4,3},{5,4},{6,5},{7,6},{8,7},{9,8},{10,9},{11,1... | collective-permute-start | bytes 147464 | tf_op jit(solution)/shard_map/ppermute | solution.py:18
  210.7 7.2 %collective-permute-start.14 = (f32[3,2,1,4,4,128]{5,4,3,2,1,0:T(4,128)S(1)}, f32[3,2,1,4,4,128]{5,4,3,2,1,0:T(4,128)S(1)}, u32[]{:S(2)}, u32[]{:S(2)}) collective-permute-start(f32[3,2,1,4,4,128]{5,4,3,2,1,0:T(4,128)S(1)} %get-tuple-element.238), channel_id=1, source_target_pairs={{0,1},{1,2},{2,3},{3,4},{4,5},{5,6},{6,7},{7,8},{8,9},{9,10},{10,1... | collective-permute-start | bytes 147464 | tf_op jit(solution)/shard_map/ppermute | solution.py:17
  218.6 9.5 %collective-permute-start.17 = (f32[3,2,1,4,4,128]{5,4,3,2,1,0:T(4,128)S(1)}, f32[3,2,1,4,4,128]{5,4,3,2,1,0:T(4,128)S(1)}, u32[]{:S(2)}, u32[]{:S(2)}) collective-permute-start(f32[3,2,1,4,4,128]{5,4,3,2,1,0:T(4,128)S(1)} %get-tuple-element.237), channel_id=1, source_target_pairs={{1,0},{2,1},{3,2},{4,3},{5,4},{6,5},{7,6},{8,7},{9,8},{10,9},{11,1... | collective-permute-start | bytes 147464 | tf_op jit(solution)/shard_map/ppermute | solution.py:18
  219.9 8.2 %collective-permute-start.16 = (f32[3,2,1,4,4,128]{5,4,3,2,1,0:T(4,128)S(1)}, f32[3,2,1,4,4,128]{5,4,3,2,1,0:T(4,128)S(1)}, u32[]{:S(2)}, u32[]{:S(2)}) collective-permute-start(f32[3,2,1,4,4,128]{5,4,3,2,1,0:T(4,128)S(1)} %get-tuple-element.236), channel_id=1, source_target_pairs={{0,1},{1,2},{2,3},{3,4},{4,5},{5,6},{6,7},{7,8},{8,9},{9,10},{10,1... | collective-permute-start | bytes 147464 | tf_op jit(solution)/shard_map/ppermute | solution.py:17
  223.4 5.2 %collective-permute-start.26 = (f32[2,1,4,12,256]{4,2,3,1,0:T(4,128)S(1)}, f32[2,1,4,12,256]{4,2,3,1,0:T(4,128)S(1)}, u32[]{:S(2)}, u32[]{:S(2)}) collective-permute-start(f32[2,1,4,12,256]{4,2,3,1,0:T(4,128)S(1)} %get-tuple-element.212), channel_id=1, source_target_pairs={{0,1},{1,2},{2,3},{3,4},{4,5},{5,6},{6,7},{7,8},{8,9},{9,10},{10,1... | collective-permute-start | bytes 294920 | tf_op jit(solution)/shard_map/ppermute | solution.py:17
  226.8 3.2 collective-permute-start.27
  232.2 59.0 %all-to-all-start.4 = ((f32[2,1,4,256]{2,0,1,3:T(2,128)}), f32[2,1,4,256]{2,0,1,3:T(2,128)S(1)}, u32[]{:S(2)}, u32[]{:S(2)}) async-start(f32[2,1,4,256]{2,0,1,3:T(2,128)} %copy.981), calls=%async_computation.4 | async-start | bytes 524288 | tf_op jit(solution)/shard_map/all_to_all | solution.py:159
  286.8 21.9 %collective-permute-start.28 = (f32[2,1,4,12,256]{4,2,3,1,0:T(4,128)S(1)}, f32[2,1,4,12,256]{4,2,3,1,0:T(4,128)S(1)}, u32[]{:S(2)}, u32[]{:S(2)}) collective-permute-start(f32[2,1,4,12,256]{4,2,3,1,0:T(4,128)S(1)} %fusion.1106), channel_id=1, source_target_pairs={{1,0},{2,1},{3,2},{4,3},{5,4},{6,5},{7,6},{8,7},{9,8},{10,9},{11,1... | collective-permute-start | bytes 294920 | tf_op jit(solution)/shard_map/ppermute | solution.py:18
  288.1 20.6 %collective-permute-start.29 = (f32[2,1,4,12,256]{4,2,3,1,0:T(4,128)S(1)}, f32[2,1,4,12,256]{4,2,3,1,0:T(4,128)S(1)}, u32[]{:S(2)}, u32[]{:S(2)}) collective-permute-start(f32[2,1,4,12,256]{4,2,3,1,0:T(4,128)S(1)} %fusion.1106), channel_id=1, source_target_pairs={{0,1},{1,2},{2,3},{3,4},{4,5},{5,6},{6,7},{7,8},{8,9},{9,10},{10,1... | collective-permute-start | bytes 294920 | tf_op jit(solution)/shard_map/ppermute | solution.py:17
  292.6 14.4 %all-to-all-start.6 = ((f32[2,1,128,8]{3,0,1,2:T(2,128)}), f32[2,1,128,8]{3,0,1,2:T(2,128)S(1)}, u32[]{:S(2)}, u32[]{:S(2)}) async-start(f32[2,1,128,8]{3,0,1,2:T(2,128)} %copy.992), calls=%async_computation.6 | async-start | bytes 262144 | tf_op jit(solution)/shard_map/all_to_all | solution.py:131
  298.9 8.4 %collective-permute-start.23 = (f32[3,2,1,4,4,128]{5,4,3,2,1,0:T(4,128)S(1)}, f32[3,2,1,4,4,128]{5,4,3,2,1,0:T(4,128)S(1)}, u32[]{:S(2)}, u32[]{:S(2)}) collective-permute-start(f32[3,2,1,4,4,128]{5,4,3,2,1,0:T(4,128)S(1)} %get-tuple-element.235), channel_id=1, source_target_pairs={{1,0},{2,1},{3,2},{4,3},{5,4},{6,5},{7,6},{8,7},{9,8},{10,9},{11,1... | collective-permute-start | bytes 147464 | tf_op jit(solution)/shard_map/ppermute | solution.py:18
  300.2 7.2 %collective-permute-start.22 = (f32[3,2,1,4,4,128]{5,4,3,2,1,0:T(4,128)S(1)}, f32[3,2,1,4,4,128]{5,4,3,2,1,0:T(4,128)S(1)}, u32[]{:S(2)}, u32[]{:S(2)}) collective-permute-start(f32[3,2,1,4,4,128]{5,4,3,2,1,0:T(4,128)S(1)} %get-tuple-element.234), channel_id=1, source_target_pairs={{0,1},{1,2},{2,3},{3,4},{4,5},{5,6},{6,7},{7,8},{8,9},{9,10},{10,1... | collective-permute-start | bytes 147464 | tf_op jit(solution)/shard_map/ppermute | solution.py:17
  309.1 4.1 %collective-permute-start.30 = (f32[2,1,4,12,256]{4,2,3,1,0:T(4,128)S(1)}, f32[2,1,4,12,256]{4,2,3,1,0:T(4,128)S(1)}, u32[]{:S(2)}, u32[]{:S(2)}) collective-permute-start(f32[2,1,4,12,256]{4,2,3,1,0:T(4,128)S(1)} %get-tuple-element.204), channel_id=1, source_target_pairs={{0,1},{1,2},{2,3},{3,4},{4,5},{5,6},{6,7},{7,8},{8,9},{9,10},{10,1... | collective-permute-start | bytes 294920 | tf_op jit(solution)/shard_map/ppermute | solution.py:17
  311.2 3.9 %collective-permute-start.31 = (f32[2,1,4,12,256]{4,2,3,1,0:T(4,128)S(1)}, f32[2,1,4,12,256]{4,2,3,1,0:T(4,128)S(1)}, u32[]{:S(2)}, u32[]{:S(2)}) collective-permute-start(f32[2,1,4,12,256]{4,2,3,1,0:T(4,128)S(1)} %get-tuple-element.204), channel_id=1, source_target_pairs={{1,0},{2,1},{3,2},{4,3},{5,4},{6,5},{7,6},{8,7},{9,8},{10,9},{11,1... | collective-permute-start | bytes 294920 | tf_op jit(solution)/shard_map/ppermute | solution.py:18
where the time goes:
time: 369 us; the launch traced here: 367 us
  blocking collectives  168 us (46%)
  starting transfers between devices  136 us (37%)
  waiting for transfers between devices  21 us (6%)
  other arithmetic  18.8 us (5%)
  local copies, waits for them, and re-layouts  14.5 us (4%)
  between operations  5.44 us (1%)
    psum x4, blocking collectives, on_device(): recorded = lax.psum(partial_record, 'gx')  168 us
    ppermute x16, starting transfers between devices, with_halo(): before = lax.ppermute(last, axis, up)  50.7 us
    all_to_all x3, starting transfers between devices, on_device(): lax.all_to_all(floor_pressure, 'gx', split_axis=3, concat_axis=2, tiled=T...  36.3 us
    all_to_all x4, starting transfers between devices, on_device(): lax.all_to_all(jnp.transpose(vel_z[:, :, :, 0, :], (0, 1, 3, 2)), 'gx', s...  28.3 us
    ppermute x16, starting transfers between devices, with_halo(): after = lax.ppermute(first, axis, down)  20.8 us
    all_to_all x4, waiting for transfers between devices, on_device(): lax.all_to_all(jnp.transpose(vel_z[:, :, :, 0, :], (0, 1, 3, 2)), 'gx', s...  14.8 us
  transfers between devices with their start and end apart: 39, of which 8 were waited for; matrix products, arithmetic and copies ran while one was open for 5% of the time, Pallas kernels for 0%

commit v1 on v0

v1 whole, which is shorter than its diff:
```python
import functools

import jax
import jax.numpy as jnp
from jax import lax
from jax.experimental import pallas as pl
from jax.experimental.pallas import tpu as pltpu
from jax.sharding import PartitionSpec as P

COEFF = (1225.0 / 1024.0, -245.0 / 3072.0, 49.0 / 5120.0, -5.0 / 7168.0)
DT = 0.2
EXACT = lax.Precision.HIGHEST
MESH = pl.DeviceIdType.MESH


def combine(at, forward):
    total = None
    for k in range(1, 5):
        term = at(k) - at(1 - k) if forward else at(k - 1) - at(-k)
        term = COEFF[k - 1] * term
        total = term if total is None else total + term
    return total


def along_z(f, forward):
    depth = f.shape[0]
    zeros = jnp.zeros((4,) + f.shape[1:], f.dtype)
    padded = jnp.concatenate([zeros, f, zeros], axis=0)
    return combine(lambda k: padded[4 + k : 4 + k + depth], forward)


def along_x(f, forward):
    size = f.shape[-1]
    lane = lax.broadcasted_iota(jnp.int32, f.shape, f.ndim - 1)

    def at(k):
        if k == 0:
            return f
        moved = pltpu.roll(f, (-k) % size, f.ndim - 1)
        keep = lane < size - k if k > 0 else lane >= -k
        return jnp.where(keep, moved, 0.0)

    return combine(at, forward)


def along_y(f, before, after, forward):
    axis = f.ndim - 2
    rows = f.shape[axis]
    tile = rows // 2
    row = lax.broadcasted_iota(jnp.int32, f.shape, axis) % tile

    def turn(a, s):
        s = s % rows
        return a if s == 0 else pltpu.roll(a, s, axis)

    def at(k):
        if k == 0:
            return f
        if k == tile:
            return after
        if k == -tile:
            return before
        if k > 0:
            return jnp.where(row < tile - k, turn(f, -k), turn(after, tile - k))
        return jnp.where(row >= -k, turn(f, -k), turn(before, -k - tile))

    return combine(at, forward)


def kernel(
    n, steps, total_y, total_x,
    rock, water, rock_par, water_par, floor, node_x, node_y, observed, source, wavelet,
    g_lambda, g_mu, g_kappa, residuals,
    state, flow, p_cur, inj,
    sig_buf, vel_buf, uy_buf, p_buf,
    sig_in, vel_in, uy_in, p_in, rec_buf, rec_in,
    sig_s, sig_r, vel_s, vel_r, uy_s, uy_r, p_s, p_r, rec_s, rec_r,
):
    me = lax.axis_index("gx")
    nz = rock.shape[1]
    wz, rows, width = water.shape[1:]
    tile = rows // 2

    def peer(s):
        return lax.rem(me + 1 + s, n)

    barrier = pltpu.get_barrier_semaphore()

    @pl.loop(0, n - 1)
    def _(s):
        pl.semaphore_signal(barrier, inc=1, device_id={"gx": peer(s)}, device_id_type=MESH)

    state[0] = rock[0]
    state[1] = rock[1]
    state[2] = rock[2]
    state[3] = rock[3]
    state[4] = rock[5]
    state[5] = rock[7]
    sig_buf[0, 0:nz] = rock[6]
    sig_buf[0, nz : 2 * nz] = rock[4]
    sig_buf[0, 2 * nz : 3 * nz] = rock[8]
    p_buf[0, 0:wz] = water[0]
    floor_f = floor[...].astype(jnp.float32)
    p_buf[0, wz] = floor_f
    p_cur[...] = water[0]
    flow[...] = water[1:4]
    inj[...] = jnp.zeros(inj.shape, jnp.float32)
    g_lambda[...] = jnp.zeros(g_lambda.shape, jnp.float32)
    g_mu[...] = jnp.zeros(g_mu.shape, jnp.float32)
    g_kappa[...] = jnp.zeros(g_kappa.shape, jnp.float32)

    for edge, slot in ((0, 0), (n - 1, 1)):

        @pl.when(me == edge)
        def _():
            for buf in (sig_in, vel_in, uy_in, p_in):
                buf[:, slot] = jnp.zeros(buf.shape[:1] + buf.shape[2:], jnp.float32)

    pl.semaphore_wait(barrier, n - 1)

    def copies(buf, into, send, recv, t):
        to_before = pltpu.make_async_remote_copy(
            src_ref=buf.at[t], dst_ref=into.at[t, 1], send_sem=send.at[t, 0], recv_sem=recv.at[t, 1],
            device_id={"gx": jnp.maximum(me - 1, 0)}, device_id_type=MESH)
        to_after = pltpu.make_async_remote_copy(
            src_ref=buf.at[t], dst_ref=into.at[t, 0], send_sem=send.at[t, 1], recv_sem=recv.at[t, 0],
            device_id={"gx": jnp.minimum(me + 1, n - 1)}, device_id_type=MESH)
        return to_before, to_after

    def start(*which):
        to_before, to_after = copies(*which)

        @pl.when(me > 0)
        def _():
            to_before.start()

        @pl.when(me < n - 1)
        def _():
            to_after.start()

    def arrive(*which):
        to_before, to_after = copies(*which)

        @pl.when(me > 0)
        def _():
            to_after.wait_recv()

        @pl.when(me < n - 1)
        def _():
            to_before.wait_recv()

    def sent(*which):
        to_before, to_after = copies(*which)

        @pl.when(me > 0)
        def _():
            to_before.wait_send()

        @pl.when(me < n - 1)
        def _():
            to_after.wait_send()

    sig = (sig_buf, sig_in, sig_s, sig_r)
    vel = (vel_buf, vel_in, vel_s, vel_r)
    uy = (uy_buf, uy_in, uy_s, uy_r)
    prs = (p_buf, p_in, p_s, p_r)

    start(*sig, 0)
    start(*prs, 0)

    z_idx = lax.broadcasted_iota(jnp.int32, (wz, rows, width), 0)
    row_idx = lax.broadcasted_iota(jnp.int32, (rows, 1), 0)
    y_in_tile = row_idx % tile
    floor_rows = floor[...][None]
    hot_x = (lax.broadcasted_iota(jnp.int32, (node_x.shape[0], width), 1) == node_x[...]).astype(jnp.float32)

    def bottom_of(rows_f):
        return (z_idx.astype(jnp.float32) == rows_f[None] - 1.0).astype(jnp.float32)

    def velocity(t):
        arrive(*sig, t)
        b = DT * rock_par[2]
        sxy, syy, syz = (sig_buf[t, i * nz : (i + 1) * nz] for i in range(3))
        lo = [sig_in[t, 0, i * nz : (i + 1) * nz] for i in range(3)]
        hi = [sig_in[t, 1, i * nz : (i + 1) * nz] for i in range(3)]
        sxx, szz, sxz = state[3], state[4], state[5]
        vx = state[0] + b * (along_x(sxx, True) + along_y(sxy, lo[0], hi[0], False) + along_z(sxz, False))
        vel_buf[t, 0:nz] = vx
        vy = state[1] + b * (along_x(sxy, False) + along_y(syy, lo[1], hi[1], True) + along_z(syz, False))
        vel_buf[t, nz : 2 * nz] = vy
        vz = state[2] + b * (along_x(sxz, False) + along_y(syz, lo[2], hi[2], False) + along_z(szz, True))
        vel_buf[t, 2 * nz : 3 * nz] = vz
        start(*vel, t)
        state[0] = vx
        state[1] = vy
        state[2] = vz

    velocity(0)

    def step(t, carry):
        live = (z_idx < floor_rows).astype(jnp.float32)
        bottom = (z_idx == floor_rows - 1).astype(jnp.float32)
        above = (z_idx < floor_rows - 1).astype(jnp.float32)
        p = p_cur[...]
        floor_p = jnp.sum(p * bottom, axis=0)
        b = DT * water_par[1]
        ux = (flow[0] - b * along_x(p, True)) * live
        flow[0] = ux
        floor_v = state[2, 0]
        uz = (flow[2] - b * along_z(p, True)) * above + floor_v[None] * bottom
        flow[2] = uz
        arrive(*prs, t)
        p_lo = p_in[t, 0, 0:wz] + inj[0][None] * bottom_of(p_in[t, 0, wz])
        p_hi = p_in[t, 1, 0:wz] + inj[1][None] * bottom_of(p_in[t, 1, wz])
        v = (flow[1] - b * along_y(p, p_lo, p_hi, True)) * live
        flow[1] = v
        uy_buf[t] = v
        start(*uy, t)

        arrive(*vel, t)
        vx, vy, vz = state[0], state[1], state[2]
        lo = [vel_in[t, 0, i * nz : (i + 1) * nz] for i in range(3)]
        hi = [vel_in[t, 1, i * nz : (i + 1) * nz] for i in range(3)]
        lam, mu = rock_par[0], rock_par[1]

        def pair(f):
            return f[:, 0:tile] * f[:, tile:rows]

        ex = along_x(vx, False)
        ey = along_y(vy, lo[1], hi[1], False)
        ez = along_z(vz, False)
        dilation = ex + ey + ez
        lam_part = lam * dilation
        state[3] = state[3] + DT * (lam_part + 2.0 * mu * ex)
        szz = state[4] + DT * (lam_part + 2.0 * mu * ez)
        state[4] = szz
        state[4, 0] = -floor_p
        sig_buf[t + 1, nz : 2 * nz] = sig_buf[t, nz : 2 * nz] + DT * (lam_part + 2.0 * mu * ey)
        gxy = along_y(vx, lo[0], hi[0], True) + along_x(vy, True)
        sig_buf[t + 1, 0:nz] = sig_buf[t, 0:nz] + DT * mu * gxy
        gyz = along_z(vy, True) + along_y(vz, lo[2], hi[2], True)
        sig_buf[t + 1, 2 * nz : 3 * nz] = sig_buf[t, 2 * nz : 3 * nz] + DT * mu * gyz

        @pl.when(t + 1 < steps)
        def _():
            start(*sig, t + 1)

        gxz = along_z(vx, True) + along_x(vz, True)
        state[5] = state[5] + DT * mu * gxz
        g_lambda[...] += pair(dilation)
        g_mu[...] += 2.0 * (pair(ex) + pair(ey) + pair(ez)) + (pair(gxy) + pair(gxz) + pair(gyz))

        partial = along_x(flow[0], False) + along_z(flow[2], False)
        arrive(*uy, t)
        p = (p_cur[...] - DT * water_par[0] * (
            partial + along_y(flow[1], uy_in[t, 0], uy_in[t, 1], False))) * live
        y_idx = me * tile + y_in_tile
        flat = (z_idx * total_y + y_idx[None]) * total_x + lax.broadcasted_iota(jnp.int32, z_idx.shape, 2)
        hit = (flat == source[0]) & (row_idx[None] < tile)
        p = p + jnp.where(hit, wavelet[t, 0], 0.0)
        p_buf[t + 1, 0:wz] = p
        p_buf[t + 1, wz] = floor_f

        @pl.when(t + 1 < steps)
        def _():
            start(*prs, t + 1)

        surface = jnp.sum(p * bottom, axis=0)
        picked = lax.dot_general(surface, hot_x, (((1,), (1,)), ((), ())), precision=EXACT,
                                 preferred_element_type=jnp.float32)
        mine = jnp.where((node_y[...] == y_idx) & (row_idx < tile), picked, 0.0)
        rec_buf[t] = mine

        @pl.loop(0, n - 1)
        def _(s):
            pltpu.make_async_remote_copy(
                src_ref=rec_buf.at[t], dst_ref=rec_in.at[t, s], send_sem=rec_s.at[t], recv_sem=rec_r.at[t],
                device_id={"gx": peer(s)}, device_id_type=MESH).start()

        @pl.when(t + 1 < steps)
        def _():
            velocity(t + 1)

        pltpu.make_async_copy(rec_in.at[t], rec_in.at[t], rec_r.at[t]).wait()
        every = jnp.sum(rec_in[t], axis=0) + mine
        misfit = jnp.sum(every, axis=0, keepdims=True) - observed[t]
        residuals[t] = misfit
        scaled = misfit * lax.rsqrt(jnp.mean(misfit * misfit, axis=1, keepdims=True) + 1e-06)

        def injected(shift):
            y_at = (me + shift) * tile + y_in_tile
            weight = jnp.where((node_y[...] == y_at) & (row_idx >= tile), scaled, 0.0)
            return jnp.dot(weight, hot_x, precision=EXACT, preferred_element_type=jnp.float32)

        inj[0] = injected(-1)
        inj[1] = injected(1)
        p = p_buf[t + 1, 0:wz] + injected(0)[None] * bottom
        p_cur[...] = p
        g_kappa[...] += pair(p)
        return carry

    lax.fori_loop(0, steps, step, 0)

    @pl.loop(0, steps)
    def _(t):
        sent(*sig, t)
        sent(*vel, t)
        sent(*uy, t)
        sent(*prs, t)
        pltpu.make_async_copy(rec_in.at[t], rec_in.at[t], rec_s.at[t]).wait()


def on_device(
    solid_state, water_state, lame_lambda, shear_mu, solid_buoy, water_kappa, water_buoy,
    seafloor, source_cell, wavelet, receiver_column, observed,
):
    n = lax.axis_size("gx")
    fields, waves, shots, wide, nz, total_y = solid_state.shape
    total_x = wide * n
    tile, wz = water_state.shape[3:5]
    steps, nodes = observed.shape[0], observed.shape[2]
    rows = waves * tile

    packed = jnp.concatenate(
        [solid_state.reshape(fields * waves, wide, nz, total_y), lame_lambda[None], shear_mu[None], solid_buoy[None]])
    count = packed.shape[0]
    packed = packed.reshape(count, wide, nz, n, tile).transpose(3, 0, 2, 4, 1)
    packed = lax.all_to_all(packed, "gx", 0, 0, tiled=True)
    packed = packed.transpose(1, 2, 3, 0, 4).reshape(count, nz, tile, total_x)
    rock = packed[: fields * waves].reshape(fields, waves, nz, tile, total_x)
    rock = rock.transpose(0, 2, 1, 3, 4).reshape(fields, nz, rows, total_x)
    rock_par = jnp.concatenate([packed[fields * waves :]] * 2, axis=2)
    water = water_state[:, :, 0].transpose(0, 3, 1, 2, 4).reshape(4, wz, rows, total_x)
    water_par = jnp.stack([water_kappa, water_buoy]).transpose(0, 2, 1, 3)
    water_par = jnp.concatenate([water_par] * 2, axis=2)
    floor = jnp.concatenate([seafloor] * 2, axis=0)
    node_x = (receiver_column % total_x)[:, None]
    node_y = (receiver_column // total_x)[None, :]

    f32 = jnp.float32
    plane = (rows, total_x)
    vmem = pl.BlockSpec(memory_space=pltpu.VMEM)
    smem = pl.BlockSpec(memory_space=pltpu.SMEM)
    pairs = pltpu.SemaphoreType.DMA((steps, 2))
    singles = pltpu.SemaphoreType.DMA((steps,))
    grad_lambda, grad_mu, grad_kappa, residuals = pl.pallas_call(
        functools.partial(kernel, n, steps, total_y, total_x),
        out_shape=(
            jax.ShapeDtypeStruct((nz, tile, total_x), f32),
            jax.ShapeDtypeStruct((nz, tile, total_x), f32),
            jax.ShapeDtypeStruct((wz, tile, total_x), f32),
            jax.ShapeDtypeStruct((steps, 1, nodes), f32),
        ),
        in_specs=[vmem] * 8 + [smem] * 2,
        out_specs=(vmem,) * 4,
        scratch_shapes=[
            pltpu.VMEM((6, nz) + plane, f32),
            pltpu.VMEM((3, wz) + plane, f32),
            pltpu.VMEM((wz,) + plane, f32),
            pltpu.VMEM((2,) + plane, f32),
            pltpu.VMEM((steps + 1, 3 * nz) + plane, f32),
            pltpu.VMEM((steps, 3 * nz) + plane, f32),
            pltpu.VMEM((steps, wz) + plane, f32),
            pltpu.VMEM((steps + 1, wz + 1) + plane, f32),
            pltpu.VMEM((steps, 2, 3 * nz) + plane, f32),
            pltpu.VMEM((steps, 2, 3 * nz) + plane, f32),
            pltpu.VMEM((steps, 2, wz) + plane, f32),
            pltpu.VMEM((steps, 2, wz + 1) + plane, f32),
            pltpu.VMEM((steps, rows, nodes), f32),
            pltpu.VMEM((steps, n - 1, rows, nodes), f32),
            pairs, pairs, pairs, pairs, pairs, pairs, pairs, pairs, singles, singles,
        ],
        compiler_params=pltpu.CompilerParams(
            collective_id=0, has_side_effects=True, vmem_limit_bytes=56 * 1024 * 1024),
    )(rock, water, rock_par, water_par, floor, node_x, node_y, observed, source_cell, wavelet)

    grads = jnp.stack([grad_lambda, grad_mu]).reshape(2, nz, tile, n, wide).transpose(3, 0, 1, 2, 4)
    grads = lax.all_to_all(grads, "gx", 0, 0, tiled=True)
    grads = grads.transpose(1, 4, 2, 0, 3).reshape(2, wide, nz, total_y)
    return grads[0], grads[1], grad_kappa.transpose(1, 0, 2), residuals


def solution(mesh):
    placed = (
        P(None, None, "groups", "gx", None, None),
        P(None, None, "groups", "gx", None, None),
        P("gx", None, None),
        P("gx", None, None),
        P("gx", None, None),
        P("gx", None, None),
        P("gx", None, None),
        P("gx", None),
        P("groups"),
        P(None, "groups"),
        P(),
        P(None, "groups", None),
    )
    return jax.shard_map(
        on_device,
        mesh=mesh,
        in_specs=placed,
        out_specs=(
            P("gx", "groups", None),
            P("gx", "groups", None),
            P("gx", "groups", None),
            P(None, "groups", None),
        ),
        check_vma=False,
    )
```

time: 369 us -> 146 us (0.40)
  blocking collectives: 168 us -> 0 us
  starting transfers between devices: 136 us -> 12.6 us
  Pallas kernels: 0 us -> 58.2 us
  local copies, waits for them, and re-layouts: 14.5 us -> 46.7 us
  other arithmetic: 18.8 us -> 11.1 us
  waiting for transfers between devices: 21 us -> 14.6 us
  between operations: 5.44 us -> 1.52 us
    psum x4 -> x0, blocking collectives: 168 us -> none  [on_device(): recorded = lax.psum(partial_record, 'gx')]
    ppermute x32 -> x0, starting transfers between devices: 71.5 us -> none  [the longest x16 50.7 us: with_halo(): before = lax.ppermute(last, axis, up)]
    pallas_call x0 -> x1, Pallas kernels: none -> 58.2 us  [on_device(): pl.pallas_call(functools.partial(kernel, n, steps, total_y, total_x), out...]
    all_to_all x7 -> x2, starting transfers between devices: 64.5 us -> 12.6 us  [the longest x1 7.3 us: on_device(): packed = lax.all_to_all(packed, 'gx', 0, 0, tiled=True)]
    unnamed x34 -> x31, local copies, waits for them, and re-layouts: 4.22 us -> 17.7 us
    slice x13 -> x7, local copies, waits for them, and re-layouts: 1.54 us -> 11.3 us  [the longest x3 5.79 us: on_device(): rock_par = jnp.concatenate([packed[fields * waves:]] * 2, axis=2)]
    add x34 -> x0, other arithmetic: 7.85 us -> none  [the longest x1 1.37 us: on_device(): grad_kappa = grad_kappa + jnp.sum(pressure[0] * pressure[1], axis=0)]
    transpose x0 -> x3, other arithmetic: none -> 6.36 us  [the longest x1 6.3 us: on_device(): packed = packed.reshape(count, wide, nz, n, tile).transpose(3, 0, 2, 4, 1)]
  transfers between devices with their start and end apart: 39 -> 2, of which waited for: 8 -> 2; matrix products, arithmetic and copies ran while one was open for 5% -> 3% of each run, Pallas kernels for 0% -> 0%
where the time goes in v1:
time: 146 us; the launch traced here: 145 us
  Pallas kernels  58.2 us (40%)
  local copies, waits for them, and re-layouts  46.7 us (32%)
  waiting for transfers between devices  14.6 us (10%)
  starting transfers between devices  12.6 us (9%)
  other arithmetic  11.1 us (8%)
  between operations  1.52 us (1%)
    pallas_call x1, Pallas kernels, on_device(): pl.pallas_call(functools.partial(kernel, n, steps, total_y, total_x), out...  58.2 us
    unnamed x31, local copies, waits for them, and re-layouts  17.7 us
    all_to_all x1, waiting for transfers between devices, on_device(): packed = lax.all_to_all(packed, 'gx', 0, 0, tiled=True)  7.39 us
    all_to_all x1, starting transfers between devices, on_device(): packed = lax.all_to_all(packed, 'gx', 0, 0, tiled=True)  7.3 us
    all_to_all x1, waiting for transfers between devices, on_device(): grads = lax.all_to_all(grads, 'gx', 0, 0, tiled=True)  7.25 us
    transpose x1, local copies, waits for them, and re-layouts, on_device(): packed = packed.reshape(count, wide, nz, n, tile).transpose(3, 0, 2, 4, 1)  6.53 us
    transpose x1, other arithmetic, on_device(): packed = packed.reshape(count, wide, nz, n, tile).transpose(3, 0, 2, 4, 1)  6.3 us
    slice x3, local copies, waits for them, and re-layouts, on_device(): rock_par = jnp.concatenate([packed[fields * waves:]] * 2, axis=2)  5.79 us
  transfers between devices with their start and end apart: 2, of which 2 were waited for; matrix products, arithmetic and copies ran while one was open for 3% of the time, Pallas kernels for 0%

profile of v1, /device:TPU:0, one launch (start us, length us, event | category | flops | bytes accessed | tf_op | source)
XLA Modules:
  0.0 144.8 jit_solution(9058973015611932220)
XLA Ops:
  0.6 0.8 copy.65
  1.5 0.8 copy.64
  2.3 0.8 copy.63
  3.2 3.8 %copy.62 = f32[9,2,1,8,4,128]{3,5,4,1,0,2:T(8,128)} copy(f32[9,2,1,8,4,128]{5,4,3,2,1,0:T(4,128)} %param.12) | data formatting | bytes 589824 | tf_op args[0]
  7.0 6.3 %maximum_bitcast_fusion = f32[32,21,4,4,8]{4,3,0,2,1:T(4,128)} fusion(f32[1,8,4,32,4]{1,4,3,2,0:T(4,128)S(1)} %bitcast.39, f32[1,8,4,32,4]{1,4,3,2,0:T(4,128)S(1)} %bitcast.40, f32[1,8,4,32,4]{1,4,3,2,0:T(4,128)S(1)} %bitcast.41, f32[18,8,4,32,4]{1,4,3,2,0:T(4,128)} %bitcast.35), kind=kLoop, calls=%fused_computation | loop fusion | flops 258048 | bytes 688128 | tf_op jit(solution)/shard_map/transpose | solution.py:327
  13.3 0.0 copy-start.1
  13.3 0.0 copy-start.8
  13.3 0.0 copy-start.7
  13.3 0.0 copy-start.5
  13.3 0.0 copy-start.3
  13.3 0.0 copy-start.4
  13.3 6.5 %copy.66 = f32[32,21,4,4,8]{1,4,3,2,0:T(8,128)S(1)} copy(f32[32,21,4,4,8]{4,3,0,2,1:T(4,128)} %maximum_bitcast_fusion) | data formatting | bytes 688128 | tf_op jit(solution)/shard_map/transpose | solution.py:327
  19.8 2.6 %reshape.44 = f32[32,1,2688]{2,1,0:T(1,128)} reshape(f32[32,4,4,8,21]{4,3,2,1,0:T(8,128)S(1)} %bitcast.36) | data formatting | bytes 688128
  22.5 7.3 %all-to-all-start = ((f32[32,1,2688]{2,1,0:T(1,128)}), f32[32,1,2688]{2,1,0:T(1,128)S(1)}, u32[]{:S(2)}, u32[]{:S(2)}) async-start(f32[32,1,2688]{2,1,0:T(1,128)} %reshape.44), calls=%async_computation | async-start | bytes 688128 | tf_op jit(solution)/shard_map/all_to_all | solution.py:328
  29.8 0.0 copy-done.1
  29.8 0.9 reshape.43.water
  30.7 0.0 copy-done.8
  30.7 0.5 fusion.1
  31.3 0.7 copy.71.node_x
  32.6 0.0 copy-done.7
  32.7 0.7 copy.72.wavelet
  33.3 0.0 copy-done.5
  33.3 0.6 pad_add_fusion.floor
  33.9 0.0 copy-done.3
  33.9 0.0 copy-done.4
  34.0 0.7 pad_maximum_fusion.water_par
  34.7 7.4 %all-to-all-done = f32[32,1,2688]{2,1,0:T(1,128)S(1)} async-done(((f32[32,1,2688]{2,1,0:T(1,128)}), f32[32,1,2688]{2,1,0:T(1,128)S(1)}, u32[]{:S(2)}, u32[]{:S(2)}) %all-to-all-start) | async-done | bytes 344096 | tf_op jit(solution)/shard_map/all_to_all | solution.py:328
  42.1 0.5 broadcast.24
  42.6 1.5 %reduce = f32[32,2688]{1,0:T(8,128)S(1)} reduce(f32[32,1,2688]{2,1,0:T(1,128)S(1)} %all-to-all-done, f32[]{:T(128)} %broadcast.24), dimensions={1}, to_apply=%all_to_all.6.reduce_sub_computation | reduce | bytes 688132 | tf_op jit(solution)/shard_map/all_to_all | solution.py:328
  44.0 3.6 %reshape.45 = f32[32,4,4,8,21]{4,3,2,1,0:T(8,128)} reshape(f32[32,2688]{1,0:T(8,128)S(1)} %reduce) | data formatting | bytes 688128
  47.7 1.8 %bitcast_bitcast_fusion = f32[21,4,4,32,8]{0,4,2,1,3:T(8,128)S(1)} fusion(f32[32,4,4,8,21]{4,3,2,1,0:T(8,128)} %reshape.45), kind=kLoop, calls=%fused_computation.14 | loop fusion | bytes 688128 | tf_op jit(solution)/shard_map/transpose | solution.py:329
  49.5 2.0 %slice.24 = f32[3,4,4,32,8]{0,4,2,1,3:T(8,128)} slice(f32[21,4,4,32,8]{0,4,2,1,3:T(8,128)S(1)} %bitcast_bitcast_fusion), slice={[18:21], [0:4], [0:4], [0:32], [0:8]} | slice | bytes 98304 | tf_op jit(solution)/shard_map/slice | solution.py:332
  51.5 5.4 %copy.67 = f32[18,4,4,32,8]{4,3,2,1,0:T(8,128)} copy(f32[18,4,4,32,8]{0,4,2,1,3:T(8,128)S(1)} %bitcast.34) | data formatting | bytes 589824 | tf_op jit(solution)/shard_map/slice | solution.py:330
  56.9 0.0 copy-start
  56.9 4.3 %reshape.41 = f32[9,2,4,4,256]{4,3,2,1,0:T(4,128)S(1)} reshape(f32[18,4,4,32,8]{4,3,2,1,0:T(8,128)} %copy.67) | data formatting | bytes 589824 | tf_op jit(solution)/shard_map/reshape | solution.py:330
  61.2 0.8 reshape.42.rock
  62.0 0.0 copy-done
  62.0 3.4 %copy.70 = f32[3,4,4,32,8]{4,3,2,1,0:T(8,128)S(1)} copy(f32[3,4,4,32,8]{0,4,2,1,3:T(8,128)S(1)} %copy-done) | data formatting | bytes 98304 | tf_op jit(solution)/shard_map/slice | solution.py:332
  65.4 0.4 slice.20
  65.8 0.7 pad_maximum_fusion.1.rock_par
  66.5 58.2 %shard_map.147 = (f32[4,4,256]{2,1,0:T(4,128)}, f32[4,4,256]{2,1,0:T(4,128)}, f32[12,4,256]{2,1,0:T(4,128)}, f32[4,1,128]{2,1,0:T(1,128)}) custom-call(f32[9,4,8,256]{3,2,1,0:T(8,128)} %reshape.42.rock, f32[4,12,8,256]{3,2,1,0:T(8,128)} %reshape.43.water, f32[3,4,8,256]{3,2,1,0:T(8,128)} %pad_maximum_fusion.1.rock_par, ...), custom_call_target="tpu_custom_call" | custom-call | tf_op jit(solution)/shard_map/pallas_call | solution.py:346
  124.7 0.0 copy-start.2
  124.7 0.0 copy-start.6
  124.7 0.9 stack.22
  125.6 0.9 stack.21
  126.5 0.3 copy.73
  126.9 1.2 reshape.46
  128.0 5.3 %all-to-all-start.1 = ((f32[32,1,256]{2,1,0:T(1,128)}), f32[32,1,256]{2,1,0:T(1,128)S(1)}, u32[]{:S(2)}, u32[]{:S(2)}) async-start(f32[32,1,256]{2,1,0:T(1,128)} %reshape.46), calls=%async_computation.1 | async-start | bytes 65536 | tf_op jit(solution)/shard_map/all_to_all | solution.py:378
  133.4 7.2 %all-to-all-done.1 = f32[32,1,256]{2,1,0:T(1,128)S(1)} async-done(((f32[32,1,256]{2,1,0:T(1,128)}), f32[32,1,256]{2,1,0:T(1,128)S(1)}, u32[]{:S(2)}, u32[]{:S(2)}) %all-to-all-start.1) | async-done | bytes 32800 | tf_op jit(solution)/shard_map/all_to_all | solution.py:378
  140.6 0.7 reduce.1
  141.3 0.7 reshape.47
  142.1 0.7 copy.76
  142.8 0.7 copy.77
  143.6 0.0 copy-done.2
  143.6 0.6 copy.81
  144.2 0.0 copy-done.6
  144.2 0.6 copy.82
  (7 shorter events, 0.2 us)
Async XLA Ops:
  13.3 16.5 %copy-start.1 = (f32[4,2,1,4,12,256]{5,3,4,2,1,0:T(4,128)S(1)}, f32[4,2,1,4,12,256]{5,3,4,2,1,0:T(4,128)}, u32[]{:S(2)}) copy-start(f32[4,2,1,4,12,256]{5,3,4,2,1,0:T(4,128)} %param.13) | copy-start | bytes 1179652
  13.3 17.5 %copy-start.8 = (s32[128]{0:T(128)S(1)}, s32[128]{0:T(128)}, u32[]{:S(2)}) copy-start(s32[128]{0:T(128)} %param.22) | copy-start | bytes 1540
  13.3 19.4 %copy-start.7 = (f32[4,1]{0,1:T(1,128)S(1)}, f32[4,1]{0,1:T(1,128)}, u32[]{:S(2)}) copy-start(f32[4,1]{0,1:T(1,128)} %param.21) | copy-start | bytes 52
  13.3 20.1 %copy-start.5 = (s32[4,256]{1,0:T(4,128)S(1)}, s32[4,256]{1,0:T(4,128)}, u32[]{:S(2)}) copy-start(s32[4,256]{1,0:T(4,128)} %param.19) | copy-start | bytes 12292
  13.3 20.7 %copy-start.3 = (f32[4,12,256]{2,0,1:T(4,128)S(1)}, f32[4,12,256]{2,0,1:T(4,128)}, u32[]{:S(2)}) copy-start(f32[4,12,256]{2,0,1:T(4,128)} %param.18) | copy-start | bytes 147460
  13.3 20.6 %copy-start.4 = (f32[4,12,256]{2,0,1:T(4,128)S(1)}, f32[4,12,256]{2,0,1:T(4,128)}, u32[]{:S(2)}) copy-start(f32[4,12,256]{2,0,1:T(4,128)} %param.17) | copy-start | bytes 147460
  22.5 19.6 %all-to-all-start = ((f32[32,1,2688]{2,1,0:T(1,128)}), f32[32,1,2688]{2,1,0:T(1,128)S(1)}, u32[]{:S(2)}, u32[]{:S(2)}) async-start(f32[32,1,2688]{2,1,0:T(1,128)} %reshape.44), calls=%async_computation | async-start | bytes 688128 | tf_op jit(solution)/shard_map/all_to_all | solution.py:328
  56.9 5.1 %copy-start = (f32[3,4,4,32,8]{0,4,2,1,3:T(8,128)S(1)}, f32[3,4,4,32,8]{0,4,2,1,3:T(8,128)}, u32[]{:S(2)}) copy-start(f32[3,4,4,32,8]{0,4,2,1,3:T(8,128)} %slice.24) | copy-start | bytes 147460
  124.7 18.9 %copy-start.2 = (f32[12,4,256]{2,1,0:T(4,128)S(1)}, f32[12,4,256]{2,1,0:T(4,128)}, u32[]{:S(2)}) copy-start(f32[12,4,256]{2,1,0:T(4,128)} %get-tuple-element.10) | copy-start | bytes 147460
  124.7 19.5 %copy-start.6 = (f32[4,1,128]{2,1,0:T(1,128)S(1)}, f32[4,1,128]{2,1,0:T(1,128)}, u32[]{:S(2)}) copy-start(f32[4,1,128]{2,1,0:T(1,128)} %get-tuple-element.35) | copy-start | bytes 6148
  128.0 12.6 %all-to-all-start.1 = ((f32[32,1,256]{2,1,0:T(1,128)}), f32[32,1,256]{2,1,0:T(1,128)S(1)}, u32[]{:S(2)}, u32[]{:S(2)}) async-start(f32[32,1,256]{2,1,0:T(1,128)} %reshape.46), calls=%async_computation.1 | async-start | bytes 65536 | tf_op jit(solution)/shard_map/all_to_all | solution.py:378

commit v2 on v1

--- a/solution.py
+++ b/solution.py
@@ -9,7 +9,6 @@
 
 COEFF = (1225.0 / 1024.0, -245.0 / 3072.0, 49.0 / 5120.0, -5.0 / 7168.0)
 DT = 0.2
-EXACT = lax.Precision.HIGHEST
 MESH = pl.DeviceIdType.MESH
 
 
@@ -67,19 +66,33 @@
     return combine(at, forward)
 
 
+def exact_dot(a, hot, dims):
+    high = a.astype(jnp.bfloat16).astype(jnp.float32)
+    rest = a - high
+    middle = rest.astype(jnp.bfloat16).astype(jnp.float32)
+    split = jnp.concatenate([high, middle, rest - middle], axis=0).astype(jnp.bfloat16)
+    out = lax.dot_general(split, hot, (dims, ((), ())), preferred_element_type=jnp.float32)
+    m = a.shape[0]
+    return out[0:m] + (out[m : 2 * m] + out[2 * m :])
+
+
 def kernel(
     n, steps, total_y, total_x,
-    rock, water, rock_par, water_par, floor, node_x, node_y, observed, source, wavelet,
-    g_lambda, g_mu, g_kappa, residuals,
-    state, flow, p_cur, inj,
+    solid, water, lame, mu_ref, buoy, kappa, wbuoy, floor_ref, nodes, observed, source, wavelet,
+    out_lambda, out_mu, out_kappa, residuals,
+    state, rock_par, flow, water_par, p_cur, inj,
+    g_lambda, g_mu, g_kappa,
+    rows_x, pack_out, pack_in, pack_all, grad_out, grad_in, grad_rows,
     sig_buf, vel_buf, uy_buf, p_buf,
     sig_in, vel_in, uy_in, p_in, rec_buf, rec_in,
-    sig_s, sig_r, vel_s, vel_r, uy_s, uy_r, p_s, p_r, rec_s, rec_r,
+    sig_s, sig_r, vel_s, vel_r, uy_s, uy_r, p_s, p_r, rec_s, rec_r, all_s, all_r,
 ):
     me = lax.axis_index("gx")
-    nz = rock.shape[1]
-    wz, rows, width = water.shape[1:]
-    tile = rows // 2
+    wide, nz = lame.shape[0:2]
+    wz, width = kappa.shape[1:]
+    tile = kappa.shape[0]
+    rows = 2 * tile
+    f32 = jnp.float32
 
     def peer(s):
         return lax.rem(me + 1 + s, n)
@@ -90,33 +103,51 @@
     def _(s):
         pl.semaphore_signal(barrier, inc=1, device_id={"gx": peer(s)}, device_id_type=MESH)
 
-    state[0] = rock[0]
-    state[1] = rock[1]
-    state[2] = rock[2]
-    state[3] = rock[3]
-    state[4] = rock[5]
-    state[5] = rock[7]
-    sig_buf[0, 0:nz] = rock[6]
-    sig_buf[0, nz : 2 * nz] = rock[4]
-    sig_buf[0, 2 * nz : 3 * nz] = rock[8]
-    p_buf[0, 0:wz] = water[0]
-    floor_f = floor[...].astype(jnp.float32)
+    rows_x[...] = jnp.zeros(rows_x.shape, f32)
+    for wave in range(2):
+        for field in range(9):
+            at = wave * 10 * nz + field * nz
+            rows_x[:, at : at + nz, :] = solid[field, wave, 0]
+    for i, ref in enumerate((lame, mu_ref, buoy)):
+        at = (20 + i) * nz
+        rows_x[:, at : at + nz, :] = ref[...]
+    lane = lax.broadcasted_iota(jnp.int32, (total_y, 128), 1)
+    y_of = lax.broadcasted_iota(jnp.int32, (total_y, 128), 0) % tile
+    for x in range(wide):
+        t0 = jnp.transpose(rows_x[x])
+        t1, t2 = (pltpu.roll(t0, total_y - k, 0) for k in (1, 2))
+        half = jnp.where(lane < 64, t0, pltpu.roll(t1, 64, 1))
+        tb = pltpu.roll(t0, 1, 0)
+        quarter = jnp.where(
+            lane < 32, pltpu.roll(tb, 64, 1),
+            jnp.where(lane < 64, pltpu.roll(t0, 96, 1), jnp.where(lane < 96, t1, pltpu.roll(t2, 32, 1))))
+        pack_out[:, x, :] = jnp.where(y_of == 1, quarter, half)
+
+    for wave in range(2):
+        for y in range(tile):
+            at = wave * tile + y
+            p_buf[0, 0:wz, at, :] = water[0, wave, 0, y]
+    floor = jnp.concatenate([floor_ref[...], floor_ref[...]], axis=0)
+    floor_f = floor.astype(f32)
     p_buf[0, wz] = floor_f
-    p_cur[...] = water[0]
-    flow[...] = water[1:4]
-    inj[...] = jnp.zeros(inj.shape, jnp.float32)
-    g_lambda[...] = jnp.zeros(g_lambda.shape, jnp.float32)
-    g_mu[...] = jnp.zeros(g_mu.shape, jnp.float32)
-    g_kappa[...] = jnp.zeros(g_kappa.shape, jnp.float32)
 
     for edge, slot in ((0, 0), (n - 1, 1)):
 
         @pl.when(me == edge)
         def _():
             for buf in (sig_in, vel_in, uy_in, p_in):
-                buf[:, slot] = jnp.zeros(buf.shape[:1] + buf.shape[2:], jnp.float32)
+                buf[:, slot] = jnp.zeros(buf.shape[:1] + buf.shape[2:], f32)
 
     pl.semaphore_wait(barrier, n - 1)
+
+    @pl.loop(0, n - 1)
+    def _(s):
+        pltpu.make_async_remote_copy(
+            src_ref=pack_out.at[pl.ds(peer(s) * tile, 3)], dst_ref=pack_in.at[s],
+            send_sem=all_s.at[0], recv_sem=all_r.at[0],
+            device_id={"gx": peer(s)}, device_id_type=MESH).start()
+
+    pack_in[n - 1] = pack_out[pl.ds(me * tile, 3)]
 
     def copies(buf, into, send, recv, t):
         to_before = pltpu.make_async_remote_copy(
@@ -165,14 +196,51 @@
     uy = (uy_buf, uy_in, uy_s, uy_r)
     prs = (p_buf, p_in, p_s, p_r)
 
+    start(*prs, 0)
+
+    for wave in range(2):
+        for y in range(tile):
+            at = wave * tile + y
+            for i in range(3):
+                flow[i, :, at, :] = water[i + 1, wave, 0, y]
+            water_par[0, :, at, :] = kappa[y]
+            water_par[1, :, at, :] = wbuoy[y]
+    p_cur[...] = p_buf[0, 0:wz]
+    inj[...] = jnp.zeros(inj.shape, f32)
+    g_lambda[...] = jnp.zeros(g_lambda.shape, f32)
+    g_mu[...] = jnp.zeros(g_mu.shape, f32)
+    g_kappa[...] = jnp.zeros(g_kappa.shape, f32)
+
+    first = pl.ds(0, n - 1)
+    pltpu.make_async_copy(pack_in.at[first], pack_in.at[first], all_r.at[0]).wait()
+
+    @pl.loop(0, n)
+    def _(src):
+        pack_all[:, src] = pack_in[lax.rem(me - 1 - src + 2 * n, n)]
+
+    whole = [jnp.transpose(pack_all[i].reshape(total_x, 128)) for i in range(3)]
+    for y in range(tile):
+        large = whole[0 if y < 2 else 2][(y % 2) * 64 : (y % 2) * 64 + 64]
+        every = jnp.concatenate([large, whole[1][y * 32 : y * 32 + 32]], axis=0)
+        for wave in range(2):
+            at = wave * 10 * nz
+            part = every[at : at + 9 * nz]
+            for to, field in ((0, 0), (1, 1), (2, 2), (3, 3), (4, 5), (5, 7)):
+                state[to, :, wave * tile + y, :] = part[field * nz : (field + 1) * nz]
+            for to, field in enumerate((6, 4, 8)):
+                sig_buf[0, to * nz : (to + 1) * nz, wave * tile + y, :] = part[field * nz : (field + 1) * nz]
+            for i in range(3):
+                rock_par[i, :, wave * tile + y, :] = every[(20 + i) * nz : (21 + i) * nz]
+
     start(*sig, 0)
-    start(*prs, 0)
 
     z_idx = lax.broadcasted_iota(jnp.int32, (wz, rows, width), 0)
     row_idx = lax.broadcasted_iota(jnp.int32, (rows, 1), 0)
     y_in_tile = row_idx % tile
-    floor_rows = floor[...][None]
-    hot_x = (lax.broadcasted_iota(jnp.int32, (node_x.shape[0], width), 1) == node_x[...]).astype(jnp.float32)
+    floor_rows = floor[None]
+    node_x = nodes[...] % total_x
+    node_y = nodes[...] // total_x
+    hot_x = (lax.broadcasted_iota(jnp.int32, (width, nodes.shape[1]), 0) == node_x).astype(jnp.bfloat16)
 
     def bottom_of(rows_f):
         return (z_idx.astype(jnp.float32) == rows_f[None] - 1.0).astype(jnp.float32)
@@ -257,7 +325,7 @@
         y_idx = me * tile + y_in_tile
         flat = (z_idx * total_y + y_idx[None]) * total_x + lax.broadcasted_iota(jnp.int32, z_idx.shape, 2)
         hit = (flat == source[0]) & (row_idx[None] < tile)
-        p = p + jnp.where(hit, wavelet[t, 0], 0.0)
+        p = p + jnp.where(hit, wavelet[pl.ds(t, 1)][None], 0.0)
         p_buf[t + 1, 0:wz] = p
         p_buf[t + 1, wz] = floor_f
 
@@ -266,9 +334,8 @@
             start(*prs, t + 1)
 
         surface = jnp.sum(p * bottom, axis=0)
-        picked = lax.dot_general(surface, hot_x, (((1,), (1,)), ((), ())), precision=EXACT,
-                                 preferred_element_type=jnp.float32)
-        mine = jnp.where((node_y[...] == y_idx) & (row_idx < tile), picked, 0.0)
+        picked = exact_dot(surface, hot_x, ((1,), (0,)))
+        mine = jnp.where((node_y == y_idx) & (row_idx < tile), picked, 0.0)
         rec_buf[t] = mine
 
         @pl.loop(0, n - 1)
@@ -287,19 +354,37 @@
         residuals[t] = misfit
         scaled = misfit * lax.rsqrt(jnp.mean(misfit * misfit, axis=1, keepdims=True) + 1e-06)
 
-        def injected(shift):
+        def weight(shift):
             y_at = (me + shift) * tile + y_in_tile
-            weight = jnp.where((node_y[...] == y_at) & (row_idx >= tile), scaled, 0.0)
-            return jnp.dot(weight, hot_x, precision=EXACT, preferred_element_type=jnp.float32)
-
-        inj[0] = injected(-1)
-        inj[1] = injected(1)
-        p = p_buf[t + 1, 0:wz] + injected(0)[None] * bottom
+            return jnp.where((node_y == y_at) & (row_idx >= tile), scaled, 0.0)
+
+        weights = jnp.concatenate([weight(-1), weight(1), weight(0)], axis=0)
+        injected = exact_dot(weights, hot_x, ((1,), (1,)))
+        inj[0] = injected[0:rows]
+        inj[1] = injected[rows : 2 * rows]
+        p = p_buf[t + 1, 0:wz] + injected[2 * rows :][None] * bottom
         p_cur[...] = p
         g_kappa[...] += pair(p)
         return carry
 
     lax.fori_loop(0, steps, step, 0)
+
+    grad_rows[...] = jnp.zeros(grad_rows.shape, f32)
+    for y in range(tile):
+        grad_rows[y * 2 * nz : y * 2 * nz + nz] = g_lambda[:, y, :]
+        grad_rows[y * 2 * nz + nz : (y + 1) * 2 * nz] = g_mu[:, y, :]
+    grad_out[...] = jnp.transpose(grad_rows[...]).reshape(n, wide, 128)
+
+    @pl.loop(0, n - 1)
+    def _(s):
+        pltpu.make_async_remote_copy(
+            src_ref=grad_out.at[peer(s)], dst_ref=grad_in.at[s],
+            send_sem=all_s.at[1], recv_sem=all_r.at[1],
+            device_id={"gx": peer(s)}, device_id_type=MESH).start()
+
+    grad_in[n - 1] = grad_out[me]
+    for y in range(tile):
+        out_kappa[y] = g_kappa[:, y, :]
 
     @pl.loop(0, steps)
     def _(t):
@@ -308,6 +393,26 @@
         sent(*uy, t)
         sent(*prs, t)
         pltpu.make_async_copy(rec_in.at[t], rec_in.at[t], rec_s.at[t]).wait()
+
+    pltpu.make_async_copy(pack_in.at[first], pack_in.at[first], all_s.at[0]).wait()
+    pltpu.make_async_copy(grad_in.at[first], grad_in.at[first], all_r.at[1]).wait()
+    by_x = [[] for _ in range(tile)]
+    column = lax.broadcasted_iota(jnp.int32, (n, total_y), 1)
+    slot = lax.broadcasted_iota(jnp.int32, (n, total_y), 0)
+    src = lax.rem(me - 1 - slot + 2 * n, n)
+    for x in range(wide):
+        turned = jnp.transpose(grad_in[:, x, :])
+        for y in range(tile):
+            by_x[y].append(turned[y * 2 * nz : (y + 1) * 2 * nz])
+    total = None
+    for y in range(tile):
+        place = (column == src * tile + y).astype(jnp.bfloat16)
+        part = exact_dot(jnp.concatenate(by_x[y], axis=0), place, ((1,), (0,)))
+        total = part if total is None else total + part
+    for x in range(wide):
+        out_lambda[x] = total[x * 2 * nz : x * 2 * nz + nz]
+        out_mu[x] = total[x * 2 * nz + nz : (x + 1) * 2 * nz]
+    pltpu.make_async_copy(grad_in.at[first], grad_in.at[first], all_s.at[1]).wait()
 
 
 def on_device(
@@ -321,43 +426,40 @@
     steps, nodes = observed.shape[0], observed.shape[2]
     rows = waves * tile
 
-    packed = jnp.concatenate(
-        [solid_state.reshape(fields * waves, wide, nz, total_y), lame_lambda[None], shear_mu[None], solid_buoy[None]])
-    count = packed.shape[0]
-    packed = packed.reshape(count, wide, nz, n, tile).transpose(3, 0, 2, 4, 1)
-    packed = lax.all_to_all(packed, "gx", 0, 0, tiled=True)
-    packed = packed.transpose(1, 2, 3, 0, 4).reshape(count, nz, tile, total_x)
-    rock = packed[: fields * waves].reshape(fields, waves, nz, tile, total_x)
-    rock = rock.transpose(0, 2, 1, 3, 4).reshape(fields, nz, rows, total_x)
-    rock_par = jnp.concatenate([packed[fields * waves :]] * 2, axis=2)
-    water = water_state[:, :, 0].transpose(0, 3, 1, 2, 4).reshape(4, wz, rows, total_x)
-    water_par = jnp.stack([water_kappa, water_buoy]).transpose(0, 2, 1, 3)
-    water_par = jnp.concatenate([water_par] * 2, axis=2)
-    floor = jnp.concatenate([seafloor] * 2, axis=0)
-    node_x = (receiver_column % total_x)[:, None]
-    node_y = (receiver_column // total_x)[None, :]
-
     f32 = jnp.float32
     plane = (rows, total_x)
     vmem = pl.BlockSpec(memory_space=pltpu.VMEM)
     smem = pl.BlockSpec(memory_space=pltpu.SMEM)
     pairs = pltpu.SemaphoreType.DMA((steps, 2))
+    ends = pltpu.SemaphoreType.DMA((2,))
     singles = pltpu.SemaphoreType.DMA((steps,))
-    grad_lambda, grad_mu, grad_kappa, residuals = pl.pallas_call(
+    return pl.pallas_call(
         functools.partial(kernel, n, steps, total_y, total_x),
         out_shape=(
-            jax.ShapeDtypeStruct((nz, tile, total_x), f32),
-            jax.ShapeDtypeStruct((nz, tile, total_x), f32),
-            jax.ShapeDtypeStruct((wz, tile, total_x), f32),
+            jax.ShapeDtypeStruct((wide, nz, total_y), f32),
+            jax.ShapeDtypeStruct((wide, nz, total_y), f32),
+            jax.ShapeDtypeStruct((tile, wz, total_x), f32),
             jax.ShapeDtypeStruct((steps, 1, nodes), f32),
         ),
-        in_specs=[vmem] * 8 + [smem] * 2,
+        in_specs=[vmem] * 10 + [smem, vmem],
         out_specs=(vmem,) * 4,
         scratch_shapes=[
             pltpu.VMEM((6, nz) + plane, f32),
+            pltpu.VMEM((3, nz) + plane, f32),
             pltpu.VMEM((3, wz) + plane, f32),
+            pltpu.VMEM((2, wz) + plane, f32),
             pltpu.VMEM((wz,) + plane, f32),
             pltpu.VMEM((2,) + plane, f32),
+            pltpu.VMEM((nz, tile, total_x), f32),
+            pltpu.VMEM((nz, tile, total_x), f32),
+            pltpu.VMEM((wz, tile, total_x), f32),
+            pltpu.VMEM((wide, 128, total_y), f32),
+            pltpu.VMEM((total_y, wide, 128), f32),
+            pltpu.VMEM((n, 3, wide, 128), f32),
+            pltpu.VMEM((3, n, wide, 128), f32),
+            pltpu.VMEM((n, wide, 128), f32),
+            pltpu.VMEM((n, wide, 128), f32),
+            pltpu.VMEM((128, total_x), f32),
             pltpu.VMEM((steps + 1, 3 * nz) + plane, f32),
             pltpu.VMEM((steps, 3 * nz) + plane, f32),
             pltpu.VMEM((steps, wz) + plane, f32),
@@ -368,16 +470,12 @@
             pltpu.VMEM((steps, 2, wz + 1) + plane, f32),
             pltpu.VMEM((steps, rows, nodes), f32),
             pltpu.VMEM((steps, n - 1, rows, nodes), f32),
-            pairs, pairs, pairs, pairs, pairs, pairs, pairs, pairs, singles, singles,
+            pairs, pairs, pairs, pairs, pairs, pairs, pairs, pairs, singles, singles, ends, ends,
         ],
         compiler_params=pltpu.CompilerParams(
             collective_id=0, has_side_effects=True, vmem_limit_bytes=56 * 1024 * 1024),
-    )(rock, water, rock_par, water_par, floor, node_x, node_y, observed, source_cell, wavelet)
-
-    grads = jnp.stack([grad_lambda, grad_mu]).reshape(2, nz, tile, n, wide).transpose(3, 0, 1, 2, 4)
-    grads = lax.all_to_all(grads, "gx", 0, 0, tiled=True)
-    grads = grads.transpose(1, 4, 2, 0, 3).reshape(2, wide, nz, total_y)
-    return grads[0], grads[1], grad_kappa.transpose(1, 0, 2), residuals
+    )(solid_state, water_state, lame_lambda, shear_mu, solid_buoy, water_kappa, water_buoy,
+      seafloor, receiver_column[None, :], observed, source_cell, wavelet)
 
 
 def solution(mesh):

time: 146 us -> 87.4 us (0.60)
  local copies, waits for them, and re-layouts: 46.7 us -> 8.71 us
  Pallas kernels: 58.2 us -> 77 us
  waiting for transfers between devices: 14.6 us -> 0 us
  starting transfers between devices: 12.6 us -> 0 us
  other arithmetic: 11.1 us -> 0 us
    pallas_call x1, Pallas kernels: 58.2 us -> 77 us  [on_device(): pl.pallas_call(functools.partial(kernel, n, steps, total_y, total_x), out...]
    all_to_all x2 -> x0, waiting for transfers between devices: 14.6 us -> none  [the longest x1 7.39 us: on_device(): packed = lax.all_to_all(packed, 'gx', 0, 0, tiled=True)]
    all_to_all x2 -> x0, starting transfers between devices: 12.6 us -> none  [the longest x1 7.3 us: on_device(): packed = lax.all_to_all(packed, 'gx', 0, 0, tiled=True)]
    slice x7 -> x0, local copies, waits for them, and re-layouts: 11.3 us -> none  [the longest x3 5.79 us: on_device(): rock_par = jnp.concatenate([packed[fields * waves:]] * 2, axis=2)]
    unnamed x31 -> x17, local copies, waits for them, and re-layouts: 17.7 us -> 7.21 us
    transpose x5 -> x0, local copies, waits for them, and re-layouts: 8.72 us -> none  [the longest x1 6.53 us: on_device(): packed = packed.reshape(count, wide, nz, n, tile).transpose(3, 0, 2, 4, 1)]
    transpose x3 -> x0, other arithmetic: 6.36 us -> none  [the longest x1 6.3 us: on_device(): packed = packed.reshape(count, wide, nz, n, tile).transpose(3, 0, 2, 4, 1)]
    reshape x3 -> x0, local copies, waits for them, and re-layouts: 5.99 us -> none  [the longest x1 4.28 us: on_device(): rock = packed[:fields * waves].reshape(fields, waves, nz, tile, total_x)]
  transfers between devices with their start and end apart: 2 -> 0, of which waited for: 2 -> 0; matrix products, arithmetic and copies ran while one was open for 3% -> 0% of each run, Pallas kernels for 0% -> 0%
where the time goes in v2:
time: 87.4 us; the launch traced here: 87 us
  Pallas kernels  77 us (88%)
  local copies, waits for them, and re-layouts  8.71 us (10%)
  between operations  1.31 us (1%)
    pallas_call x1, Pallas kernels, on_device(): pl.pallas_call(functools.partial(kernel, n, steps, total_y, total_x), out...  77 us
    unnamed x17, local copies, waits for them, and re-layouts  7.21 us

profile of v2, /device:TPU:0, one launch (start us, length us, event | category | flops | bytes accessed | tf_op | source)
XLA Modules:
  0.0 87.0 jit_solution(15225242384863999905)
XLA Ops:
  1.3 0.0 copy-start.4
  1.3 0.6 copy-done.4
  1.9 0.7 copy.19.wavelet
  2.6 0.0 copy-start
  2.6 1.4 %copy.17.kappa = f32[4,12,256]{2,1,0:T(8,128)} copy(f32[4,12,256]{2,0,1:T(4,128)} %param.17) | data formatting | bytes 98304 | tf_op args[5]
  4.0 0.0 copy-done
  4.0 0.6 copy.18.wbuoy
  4.7 1.9 %copy.16.water = f32[4,2,1,4,12,256]{5,4,3,2,1,0:T(8,128)} copy(f32[4,2,1,4,12,256]{5,3,4,2,1,0:T(4,128)} %param.13) | data formatting | bytes 786432 | tf_op args[1]
  6.5 77.0 %shard_map.147 = (f32[8,4,128]{2,1,0:T(4,128)}, f32[8,4,128]{2,1,0:T(4,128)}, f32[4,12,256]{2,1,0:T(8,128)}, f32[4,1,128]{2,1,0:T(1,128)}) custom-call(f32[9,2,1,8,4,128]{5,4,3,2,1,0:T(4,128)} %solid.1, f32[4,2,1,4,12,256]{5,4,3,2,1,0:T(8,128)} %copy.16.water, f32[8,4,128]{2,1,0:T(4,128)} %lame.1, f32[8,4,128]{2,1,0:T(4,128)} %mu_ref.1, f32[8,4,128]{2,1,0:T(4,128)} %buoy.1, ...), custom_call_target="tpu_custom_call" | custom-call | tf_op jit(solution)/shard_map/pallas_call | solution.py:436
  83.5 0.0 copy-start.2
  83.5 1.5 %copy.20 = f32[4,12,256]{2,0,1:T(4,128)} copy(f32[4,12,256]{2,1,0:T(8,128)} %get-tuple-element.6) | data formatting | bytes 98304 | tf_op jit(solution)/shard_map/pallas_call | solution.py:436
  85.0 0.0 copy-done.2
  85.0 0.0 copy-start.1
  85.0 0.6 copy.25
  85.6 0.1 copy-done.1
  85.8 0.0 copy-start.3
  85.8 0.6 copy.26
  86.4 0.1 copy-done.3
  86.4 0.6 copy.27
Async XLA Ops:
  1.3 0.7 copy-start.4
  2.6 1.4 %copy-start = (f32[4,12,256]{2,0,1:T(4,128)S(1)}, f32[4,12,256]{2,0,1:T(4,128)}, u32[]{:S(2)}) copy-start(f32[4,12,256]{2,0,1:T(4,128)} %param.18) | copy-start | bytes 147460
  83.5 1.5 %copy-start.2 = (f32[8,4,128]{2,1,0:T(4,128)S(1)}, f32[8,4,128]{2,1,0:T(4,128)}, u32[]{:S(2)}) copy-start(f32[8,4,128]{2,1,0:T(4,128)} %get-tuple-element.12) | copy-start | bytes 49156
  85.0 0.7 copy-start.1
  85.8 0.7 copy-start.3
